TPU v7x, 512 devices: a whole 4x8x8 slice. The times are simulated.
512 devices in a mesh: corpus: 64 (over x, y, core), tensor: 8 (over z).
Axes of the slice: x: 4, y: 8, z: 8, core: 2. Of those that a mesh axis runs over, the one named last changes fastest.
Arguments:
- self_query: bfloat16 [1024, 4, 4096], P('corpus', None, 'tensor'), may hold values from -24 to 24
- cross_query: bfloat16 [1024, 4, 4096], P('corpus', None, 'tensor'), may hold values from -24 to 24
- cache: bfloat16 [1024, 2, 64, 4096], P('corpus', None, None, 'tensor'), may hold values from -24 to 24
- step_kv: bfloat16 [1024, 2, 4, 4096], P('corpus', None, None, 'tensor'), may hold values from -6 to 6
- kv_length: int32 [1024], P('corpus'), may hold values from 2 to 64
- positions: int32 [1024], P('corpus'), may hold values from 125 to 4095, as said below
- corpus_kv: bfloat16 [512, 2, 128, 4096], P('corpus', None, None, 'tensor'), may hold values from -24 to 24
- neighbour_shard: int32 [1024, 4], P('corpus'), may hold values from 0 to 63, all different within a row; in each aligned block of 16 rows (0 to 15, 16 to 31, ...) at most 2 rows name the same one
- neighbour_slot: int32 [1024, 4], P('corpus'), may hold values from 0 to 7
- out_weight: bfloat16 [4096, 8192], P('tensor', 'corpus'), may hold values from -0.09375 to 0.09375
Outputs:
- self_heads: bfloat16 [1024, 4, 4096], P('corpus', None, 'tensor')
- cross_out: bfloat16 [64, 64, 8192], P('tensor', None, 'corpus')
Inputs may be any that keep to these rules, and one draw needn't show every extreme that they name: `neighbour_shard`: the (4) shards of one request are distinct; the first 2 serve the span in progress, the others the next span. Among the requests of one replica (aligned blocks of 16 requests) no shard is named more than 2 times, a bound that some block reaches. Each first decoded position lies 1 to 3 positions before a multiple of 64.
All inputs are finite; a program needn't handle non-finite values.
Results may differ from a plain program's by a relative error of at most 0.0055.
Values may be sent and summed in bfloat16 or wider, within the bound.
A program may use at most 64 MiB of HBM per device.

v0:
```python
import jax
import jax.numpy as jnp
from jax import lax
from jax.sharding import PartitionSpec as P

HDIM = 128
NBR = 2
SPAN = 64


masked_value = -1e30


def attend_self(queries, cached, fresh, lengths):
    request_count, step_count, width = queries.shape
    head_count = width // HDIM
    score_scale = HDIM ** (-0.5)
    query_heads = queries.reshape(request_count, step_count, head_count, HDIM)
    cache_keys = cached[:, 0].reshape(request_count, -1, head_count, HDIM)
    cache_values = cached[:, 1].reshape(request_count, -1, head_count, HDIM)
    fresh_keys = fresh[:, 0].reshape(request_count, step_count, head_count, HDIM)
    fresh_values = fresh[:, 1].reshape(request_count, step_count, head_count, HDIM)
    cache_scores = (
        jnp.einsum("rthd,rlhd->rthl", query_heads, cache_keys, preferred_element_type=jnp.float32)
        * score_scale
    )
    is_live = jnp.arange(cache_keys.shape[1], dtype=jnp.int32)[None, :] < lengths[:, None]
    cache_scores = jnp.where(is_live[:, None, None, :], cache_scores, masked_value)
    fresh_scores = (
        jnp.einsum("rthd,ruhd->rthu", query_heads, fresh_keys, preferred_element_type=jnp.float32)
        * score_scale
    )
    causal = jnp.arange(step_count)[None, :] <= jnp.arange(step_count)[:, None]
    fresh_scores = jnp.where(causal[None, :, None, :], fresh_scores, masked_value)
    row_max = jnp.maximum(jnp.max(cache_scores, axis=-1), jnp.max(fresh_scores, axis=-1))
    cache_exp = jnp.exp(cache_scores - row_max[..., None])
    fresh_exp = jnp.exp(fresh_scores - row_max[..., None])
    totals = jnp.sum(cache_exp, axis=-1) + jnp.sum(fresh_exp, axis=-1)
    weighted = jnp.einsum(
        "rthl,rlhd->rthd",
        cache_exp.astype(jnp.bfloat16),
        cache_values,
        preferred_element_type=jnp.float32,
    )
    weighted = weighted + jnp.einsum(
        "rthu,ruhd->rthd",
        fresh_exp.astype(jnp.bfloat16),
        fresh_values,
        preferred_element_type=jnp.float32,
    )
    return (
        (weighted / totals[..., None])
        .astype(jnp.bfloat16)
        .reshape(request_count, step_count, width)
    )


def attend_blocks(queries, tags, corpus_kv):
    source_count, item_count, step_count, width = queries.shape
    head_count = width // HDIM
    token_count = corpus_kv.shape[2]
    score_scale = HDIM ** (-0.5)
    query_heads = queries.reshape(source_count, item_count, step_count, head_count, HDIM)
    chosen = jnp.zeros((source_count, item_count, step_count, head_count, token_count), jnp.float32)
    for block_index in range(corpus_kv.shape[0]):
        block_keys = corpus_kv[block_index, 0].reshape(token_count, head_count, HDIM)
        scores = (
            jnp.einsum(
                "skthd,nhd->skthn", query_heads, block_keys, preferred_element_type=jnp.float32
            )
            * score_scale
        )
        chosen = jnp.where((tags == block_index + 1)[:, :, None, None, None], scores, chosen)
    row_max = jnp.max(chosen, axis=-1)
    exponent = jnp.exp(chosen - row_max[..., None])
    totals = jnp.sum(exponent, axis=-1)
    weights_low = exponent.astype(jnp.bfloat16)
    value_sums = jnp.zeros((source_count, item_count, step_count, head_count, HDIM), jnp.float32)
    for block_index in range(corpus_kv.shape[0]):
        block_values = corpus_kv[block_index, 1].reshape(token_count, head_count, HDIM)
        partial_sum = jnp.einsum(
            "skthn,nhd->skthd", weights_low, block_values, preferred_element_type=jnp.float32
        )
        value_sums = jnp.where(
            (tags == block_index + 1)[:, :, None, None, None], partial_sum, value_sums
        )
    return (value_sums.reshape(source_count, item_count, step_count, width), row_max, totals)


def select_span(values, use_next):
    flags = jnp.expand_dims(use_next, 1)
    flags = flags.reshape(flags.shape + (1,) * (values.ndim - 3))
    return jnp.where(flags, values[:, NBR:], values[:, :NBR])


def on_device(
    self_query,
    cross_query,
    cache,
    step_kv,
    kv_length,
    positions,
    corpus_kv,
    neighbour_shard,
    neighbour_slot,
    out_weight,
):
    self_heads = attend_self(self_query, cache, step_kv, kv_length)
    request_count, step_count, width = cross_query.shape
    head_count = width // HDIM
    shard_count = lax.axis_size("corpus")
    slot_count = max(2, 2 * NBR * request_count // shard_count)
    item_count = request_count * 2 * NBR
    targets = neighbour_shard.reshape(item_count)
    block_places = neighbour_slot.reshape(item_count)
    same_target = targets[:, None] == targets[None, :]
    earlier = jnp.arange(item_count)[None, :] < jnp.arange(item_count)[:, None]
    item_ranks = jnp.sum(same_target & earlier, axis=1)
    places = targets * slot_count + item_ranks
    item_queries = jnp.broadcast_to(
        cross_query[:, None], (request_count, 2 * NBR, step_count, width)
    ).reshape(item_count, step_count, width)
    send_queries = (
        jnp.zeros((shard_count * slot_count, step_count, width), jnp.bfloat16)
        .at[places]
        .set(item_queries)
    )
    send_queries = send_queries.reshape(shard_count, slot_count, step_count, width)
    send_tags = (
        jnp.zeros((shard_count * slot_count,), jnp.int32)
        .at[places]
        .set(block_places + 1)
        .reshape(shard_count, slot_count)
    )
    partials = attend_blocks(
        lax.all_to_all(send_queries, "corpus", split_axis=0, concat_axis=0, tiled=True),
        lax.all_to_all(send_tags, "corpus", split_axis=0, concat_axis=0, tiled=True),
        corpus_kv,
    )
    sums_back = lax.all_to_all(partials[0], "corpus", split_axis=0, concat_axis=0, tiled=True)
    maxima_back = lax.all_to_all(partials[1], "corpus", split_axis=0, concat_axis=0, tiled=True)
    totals_back = lax.all_to_all(partials[2], "corpus", split_axis=0, concat_axis=0, tiled=True)
    item_sums = sums_back.reshape(shard_count * slot_count, step_count, width)[places]
    item_sums = item_sums.reshape(request_count, 2 * NBR, step_count, head_count, HDIM)
    item_max = maxima_back.reshape(shard_count * slot_count, step_count, head_count)[places]
    item_max = item_max.reshape(request_count, 2 * NBR, step_count, head_count)
    item_total = totals_back.reshape(shard_count * slot_count, step_count, head_count)[places]
    item_total = item_total.reshape(request_count, 2 * NBR, step_count, head_count)
    boundary = SPAN - positions % SPAN
    use_next = jnp.arange(step_count, dtype=jnp.int32)[None, :] >= boundary[:, None]
    chosen_sums = select_span(item_sums, use_next)
    chosen_max = select_span(item_max, use_next)
    chosen_total = select_span(item_total, use_next)
    joint = jnp.max(chosen_max, axis=1)
    factors = jnp.exp(chosen_max - joint[:, None])
    numer = jnp.sum(factors[..., None] * chosen_sums, axis=1)
    denom = jnp.sum(factors * chosen_total, axis=1)
    cross_heads = (numer / denom[..., None]).astype(jnp.bfloat16)
    flat_heads = cross_heads.reshape(request_count * step_count, width)
    partial_terms = jnp.einsum(
        "rcw,wd->rcd",
        lax.all_gather(flat_heads[:, None, :], "corpus", axis=1, tiled=True),
        out_weight,
        preferred_element_type=jnp.float32,
    )
    cross_out = lax.psum_scatter(partial_terms, "tensor", scatter_dimension=0, tiled=True).astype(
        jnp.bfloat16
    )
    return (self_heads, cross_out)


def solution(mesh):
    return jax.shard_map(
        on_device,
        mesh=mesh,
        in_specs=(
            P("corpus", None, "tensor"),
            P("corpus", None, "tensor"),
            P("corpus", None, None, "tensor"),
            P("corpus", None, None, "tensor"),
            P("corpus"),
            P("corpus"),
            P("corpus", None, None, "tensor"),
            P("corpus", None),
            P("corpus", None),
            P("tensor", "corpus"),
        ),
        out_specs=(P("corpus", None, "tensor"), P("tensor", None, "corpus")),
        check_vma=False,
    )
```

profile of v0, /device:TPU:1, one launch (start us, length us, event | category | flops | bytes accessed | tf_op | source)
XLA Modules:
  0.0 280.1 jit_solution(17308488218929526339)
XLA Ops:
  11.6 11.6 %all-to-all-start = ((s32[64,1,2]{2,1,0:T(1,128)}), s32[64,1,2]{2,1,0:T(1,128)S(1)}, u32[]{:S(2)}, u32[]{:S(2)}) async-start(s32[64,1,2]{2,1,0:T(1,128)} %bitcast.10), calls=%async_computation | async-start | bytes 65536 | tf_op jit(solution)/shard_map/all_to_all | solution.py:137
  25.1 7.5 %scatter_fusion = bf16[128,4,512]{2,1,0:T(4,128)(2,1)} fusion(bf16[128,4,512]{2,1,0:T(4,128)(2,1)} %broadcast_in_dim.169, s32[64]{0:T(128)S(1)} %fusion.56, bf16[64,4,512]{2,1,0:T(4,128)(2,1)S(1)} %bitcast.183), kind=kCustom, calls=%fused_computation.4 | custom fusion | bytes 786688 | tf_op jit(solution)/shard_map/scatter | solution.py:126
  33.3 10.3 %all-to-all-start.1 = ((bf16[64,2,4,512]{3,2,1,0:T(4,128)(2,1)}), bf16[64,2,4,512]{3,2,1,0:T(4,128)(2,1)S(1)}, u32[]{:S(2)}, u32[]{:S(2)}) async-start(bf16[64,2,4,512]{3,2,1,0:T(4,128)(2,1)} %bitcast.13), calls=%async_computation.1 | async-start | bytes 1048576 | tf_op jit(solution)/shard_map/all_to_all | solution.py:136
  43.6 1.1 fusion.59
  44.7 1.1 copy.478
  45.7 1.7 copy.477
  47.4 1.7 copy.476
  49.1 1.7 copy.475
  50.7 1.0 copy.479
  51.8 1.7 copy.473
  53.4 1.7 copy.472
  57.3 3.6 %all-to-all-done.1 = bf16[64,2,4,512]{3,2,1,0:T(4,128)(2,1)S(1)} async-done(((bf16[64,2,4,512]{3,2,1,0:T(4,128)(2,1)}), bf16[64,2,4,512]{3,2,1,0:T(4,128)(2,1)S(1)}, u32[]{:S(2)}, u32[]{:S(2)}) %all-to-all-start.1) | async-done | bytes 524320 | tf_op jit(solution)/shard_map/all_to_all | solution.py:136
  66.3 6.7 %all-to-all-start.4 = ((f32[64,2,4,4]{2,1,3,0:T(2,128)}), f32[64,2,4,4]{2,1,3,0:T(2,128)S(1)}, u32[]{:S(2)}, u32[]{:S(2)}) async-start(f32[64,2,4,4]{2,1,3,0:T(2,128)} %copy.409), calls=%async_computation.4 | async-start | bytes 524288 | tf_op jit(solution)/shard_map/all_to_all | solution.py:142
  76.0 9.0 %all-to-all-done.4 = f32[64,2,4,4]{2,1,3,0:T(2,128)S(1)} async-done(((f32[64,2,4,4]{2,1,3,0:T(2,128)}), f32[64,2,4,4]{2,1,3,0:T(2,128)S(1)}, u32[]{:S(2)}, u32[]{:S(2)}) %all-to-all-start.4) | async-done | bytes 8224 | tf_op jit(solution)/shard_map/all_to_all | solution.py:142
  85.0 6.0 %all-to-all-start.2 = ((f32[64,2,4,4]{3,1,2,0:T(2,128)}), f32[64,2,4,4]{3,1,2,0:T(2,128)S(1)}, u32[]{:S(2)}, u32[]{:S(2)}) async-start(f32[64,2,4,4]{3,1,2,0:T(2,128)} %copy.388), calls=%async_computation.2 | async-start | bytes 524288 | tf_op jit(solution)/shard_map/all_to_all | solution.py:141
  92.0 1.6 reshape.310
  93.6 9.4 %all-to-all-done.2 = f32[64,2,4,4]{3,1,2,0:T(2,128)S(1)} async-done(((f32[64,2,4,4]{3,1,2,0:T(2,128)}), f32[64,2,4,4]{3,1,2,0:T(2,128)S(1)}, u32[]{:S(2)}, u32[]{:S(2)}) %all-to-all-start.2) | async-done | bytes 8224 | tf_op jit(solution)/shard_map/all_to_all | solution.py:141
  103.0 6.0 %all-to-all-start.3 = ((f32[64,2,4,512]{3,2,1,0:T(4,128)}), f32[64,2,4,512]{3,2,1,0:T(4,128)S(1)}, u32[]{:S(2)}, u32[]{:S(2)}) async-start(f32[64,2,4,512]{3,2,1,0:T(4,128)} %reshape.310), calls=%async_computation.3 | async-start | bytes 2097152 | tf_op jit(solution)/shard_map/all_to_all | solution.py:140
  112.0 25.7 %all-to-all-done.3 = f32[64,2,4,512]{3,2,1,0:T(4,128)S(1)} async-done(((f32[64,2,4,512]{3,2,1,0:T(4,128)}), f32[64,2,4,512]{3,2,1,0:T(4,128)S(1)}, u32[]{:S(2)}, u32[]{:S(2)}) %all-to-all-start.3) | async-done | bytes 1048608 | tf_op jit(solution)/shard_map/all_to_all | solution.py:140
  140.0 84.9 %all-gather.2.cloned.1.call-done = bf16[64,64,512]{2,0,1:T(8,128)(2,1)} async-done(((bf16[64,1,512]{2,0,1:T(8,128)(2,1)}), bf16[64,64,512]{2,0,1:T(8,128)(2,1)}) %all-gather.2.cloned.1.call-update) | async-done | bytes 4194320 | tf_op jit(solution)/shard_map/all_gather | solution.py:162
  224.9 8.2 %fusion = f32[64,64,128]{2,1,0:T(8,128)} fusion(bf16[64,64,512]{2,0,1:T(8,128)(2,1)} %all-gather.2.cloned.1.call-done, bf16[512,128]{1,0:T(8,128)(2,1)S(1)} %copy-done), kind=kOutput, calls=%fused_computation.5 | convolution fusion | flops 536870912 | bytes 6422528 | tf_op jit(solution)/shard_map/rcw,wd->rcd/dot_general | solution.py:160
  233.2 1.7 fusion.60
  238.7 33.0 %reduce-scatter.2.cloned.1.call-done = f32[8,64,128]{2,1,0:T(8,128)} async-done(((f32[64,64,128]{2,1,0:T(8,128)}), f32[8,64,128]{2,1,0:T(8,128)}) %reduce-scatter.2.cloned.1.call-update) | async-done | bytes 262160 | tf_op jit(solution)/shard_map/reduce_scatter | solution.py:166
  271.6 1.6 convert_element_type.38
  (108 shorter events, 27.1 us)
Async XLA Ops:
  7.2 217.8 %copy-start = (bf16[512,128]{1,0:T(8,128)(2,1)S(1)}, bf16[512,128]{1,0:T(8,128)(2,1)}, u32[]{:S(2)}) copy-start(bf16[512,128]{1,0:T(8,128)(2,1)} %param.19) | copy-start | bytes 393220
  7.2 36.4 %copy-start.1 = (bf16[8,2,128,512]{3,2,1,0:T(8,128)(2,1)S(1)}, bf16[8,2,128,512]{3,2,1,0:T(8,128)(2,1)}, u32[]{:S(2)}) copy-start(bf16[8,2,128,512]{3,2,1,0:T(8,128)(2,1)} %param.16) | copy-start | bytes 6291460
  11.6 21.0 %all-to-all-start = ((s32[64,1,2]{2,1,0:T(1,128)}), s32[64,1,2]{2,1,0:T(1,128)S(1)}, u32[]{:S(2)}, u32[]{:S(2)}) async-start(s32[64,1,2]{2,1,0:T(1,128)} %bitcast.10), calls=%async_computation | async-start | bytes 65536 | tf_op jit(solution)/shard_map/all_to_all | solution.py:137
  32.7 0.6 copy-start.9
  33.3 27.6 %all-to-all-start.1 = ((bf16[64,2,4,512]{3,2,1,0:T(4,128)(2,1)}), bf16[64,2,4,512]{3,2,1,0:T(4,128)(2,1)S(1)}, u32[]{:S(2)}, u32[]{:S(2)}) async-start(bf16[64,2,4,512]{3,2,1,0:T(4,128)(2,1)} %bitcast.13), calls=%async_computation.1 | async-start | bytes 1048576 | tf_op jit(solution)/shard_map/all_to_all | solution.py:136
  44.6 11.5 %copy-start.3 = (bf16[1,1,128,512]{3,2,1,0:T(8,128)(2,1)S(1)}, bf16[1,1,128,512]{3,2,1,0:T(8,128)(2,1)}, u32[]{:S(2)}) copy-start(bf16[1,1,128,512]{3,2,1,0:T(8,128)(2,1)} %get-tuple-element.19) | copy-start | bytes 393220
  44.6 11.6 %copy-start.2 = (bf16[1,1,128,512]{3,2,1,0:T(8,128)(2,1)S(1)}, bf16[1,1,128,512]{3,2,1,0:T(8,128)(2,1)}, u32[]{:S(2)}) copy-start(bf16[1,1,128,512]{3,2,1,0:T(8,128)(2,1)} %get-tuple-element.5) | copy-start | bytes 393220
  44.7 12.5 %copy-start.10 = (s32[64,1,2]{2,1,0:T(1,128)S(1)}, s32[64,1,2]{2,1,0:T(1,128)}, u32[]{:S(2)}) copy-start(s32[64,1,2]{2,1,0:T(1,128)} %copy-done.9) | copy-start | bytes 1540
  56.5 4.9 %copy-start.4 = (bf16[1,1,128,512]{2,3,1,0:T(8,128)(2,1)S(1)}, bf16[1,1,128,512]{2,3,1,0:T(8,128)(2,1)}, u32[]{:S(2)}) copy-start(bf16[1,1,128,512]{2,3,1,0:T(8,128)(2,1)} %copy.477) | copy-start | bytes 393220
  57.3 4.5 %copy-start.5 = (bf16[1,1,128,512]{2,3,1,0:T(8,128)(2,1)S(1)}, bf16[1,1,128,512]{2,3,1,0:T(8,128)(2,1)}, u32[]{:S(2)}) copy-start(bf16[1,1,128,512]{2,3,1,0:T(8,128)(2,1)} %copy.476) | copy-start | bytes 393220
  61.4 0.9 copy-start.6
  61.7 0.9 copy-start.7
  62.1 0.9 copy-start.8
  66.3 18.7 %all-to-all-start.4 = ((f32[64,2,4,4]{2,1,3,0:T(2,128)}), f32[64,2,4,4]{2,1,3,0:T(2,128)S(1)}, u32[]{:S(2)}, u32[]{:S(2)}) async-start(f32[64,2,4,4]{2,1,3,0:T(2,128)} %copy.409), calls=%async_computation.4 | async-start | bytes 524288 | tf_op jit(solution)/shard_map/all_to_all | solution.py:142
  85.0 18.0 %all-to-all-start.2 = ((f32[64,2,4,4]{3,1,2,0:T(2,128)}), f32[64,2,4,4]{3,1,2,0:T(2,128)S(1)}, u32[]{:S(2)}, u32[]{:S(2)}) async-start(f32[64,2,4,4]{3,1,2,0:T(2,128)} %copy.388), calls=%async_computation.2 | async-start | bytes 524288 | tf_op jit(solution)/shard_map/all_to_all | solution.py:141
  92.0 17.1 %copy-start.14 = (s32[16]{0:T(128)S(1)}, s32[16]{0:T(128)}, u32[]{:S(2)}) copy-start(s32[16]{0:T(128)} %param.15) | copy-start | bytes 196
  103.0 34.6 %all-to-all-start.3 = ((f32[64,2,4,512]{3,2,1,0:T(4,128)}), f32[64,2,4,512]{3,2,1,0:T(4,128)S(1)}, u32[]{:S(2)}, u32[]{:S(2)}) async-start(f32[64,2,4,512]{3,2,1,0:T(4,128)} %reshape.310), calls=%async_computation.3 | async-start | bytes 2097152 | tf_op jit(solution)/shard_map/all_to_all | solution.py:140
  109.1 115.9 %all-gather.2.cloned.1.call-start = ((), (), s32[]{:S(2)}) async-start(), calls=%async_computation.6 | async-start | bytes 4259840 | tf_op jit(solution)/shard_map/all_gather | solution.py:162
  139.9 131.7 %reduce-scatter.2.cloned.1.call-start = ((), (), s32[]{:S(2)}) async-start(), calls=%async_computation.7 | async-start | bytes 2359296 | tf_op jit(solution)/shard_map/reduce_scatter | solution.py:166
  234.9 0.7 copy-start.11
  234.9 0.9 copy-start.12
  234.9 0.9 copy-start.13
Sparse Core Ops, SparseCore 0:
  140.1 84.8 all-gather.1
  233.3 38.3 reduce-scatter.1
where the time goes:
time: 285 us; the launch traced here: 280 us
  waiting for transfers between devices  166 us (58%)
  starting transfers between devices  40.8 us (14%)
  local copies, waits for them, and re-layouts  37.6 us (13%)
  matrix products  16.2 us (6%)
  between operations  14.5 us (5%)
  other arithmetic  5.32 us (2%)
    all_gather x1, waiting for transfers between devices, on_device(): lax.all_gather(flat_heads[:, None, :], 'corpus', axis=1, tiled=True)  84.9 us
    reduce_scatter x1, waiting for transfers between devices, on_device(): lax.psum_scatter(partial_terms, 'tensor', scatter_dimension=0, tiled=True)  33 us
    all_to_all x1, waiting for transfers between devices, on_device(): lax.all_to_all(partials[0], 'corpus', split_axis=0, concat_axis=0, tiled=...  25.7 us
    unnamed x47, local copies, waits for them, and re-layouts  14.4 us
    all_to_all x1, starting transfers between devices, on_device(): lax.all_to_all(send_tags, 'corpus', split_axis=0, concat_axis=0, tiled=True)  11.6 us
    all_to_all x1, starting transfers between devices, on_device(): lax.all_to_all(send_queries, 'corpus', split_axis=0, concat_axis=0, tiled...  10.3 us
    all_to_all x1, waiting for transfers between devices, on_device(): lax.all_to_all(partials[1], 'corpus', split_axis=0, concat_axis=0, tiled=...  9.42 us
    all_to_all x1, waiting for transfers between devices, on_device(): lax.all_to_all(partials[2], 'corpus', split_axis=0, concat_axis=0, tiled=...  9.02 us
  transfers between devices with their start and end apart: 7, of which 6 were waited for; matrix products, arithmetic and copies ran while one was open for 13% of the time, Pallas kernels for 0%

commit v1 on v0

v1 whole, which is shorter than its diff:
```python
import functools

import jax
import jax.numpy as jnp
from jax import lax
from jax.experimental import pallas as pl
from jax.experimental.pallas import tpu as pltpu
from jax.sharding import PartitionSpec as P

HDIM = 128
NBR = 2
SPAN = 64
CORES = 2
GRID_OF = {64: (4, 8), 8: (2, 2)}
MESH = pl.DeviceIdType.MESH
masked_value = -1e30
F32 = jnp.float32
BF16 = jnp.bfloat16


def pack_kernel(shard_ref, slot_ref, query_ref, send_ref, rank_ref, base, variants, total, counts):
    request_count, step_count, _ = query_ref.shape
    shard_count, message_rows, _ = send_ref.shape
    head_count = message_rows // 8
    base[...] = jnp.zeros_like(base)
    queries = query_ref[...].astype(F32)
    for head in range(head_count):
        base[:, head * 8 : head * 8 + step_count, :] = queries[:, :, head * HDIM : (head + 1) * HDIM]
    flat = base[...].reshape(request_count * message_rows, HDIM)
    row = lax.broadcasted_iota(jnp.int32, flat.shape, 0) % 8
    size = flat.shape[0]
    moved = (
        jnp.where(row < 3, flat, 0.0),
        jnp.where((row >= 3) & (row < 6), pltpu.roll(flat, 3, 0), 0.0),
        jnp.where(row < 3, pltpu.roll(flat, size - 1, 0), 0.0),
        jnp.where((row >= 3) & (row < 6), pltpu.roll(flat, 2, 0), 0.0),
    )
    for number, values in enumerate(moved):
        variants[number] = values.reshape(request_count, message_rows, HDIM)
    total[...] = jnp.zeros_like(total)

    def clear(index, carry):
        counts[index] = 0
        return carry

    lax.fori_loop(0, shard_count, clear, 0)
    tile_row = lax.broadcasted_iota(jnp.int32, (message_rows, HDIM), 0) % 8

    def place(request, carry):
        for item in range(2 * NBR):
            shard = shard_ref[request, item]
            rank = counts[shard]
            counts[shard] = rank + 1
            rank_ref[request, item] = rank
            number = rank + (2 if item >= NBR else 0)
            tag = (slot_ref[request, item] + 1).astype(F32)
            tile = jnp.where(tile_row == rank + 6, tag, variants[number, request])
            total[shard] = total[shard] + tile
        return carry

    lax.fori_loop(0, request_count, place, 0)
    send_ref[...] = total[...].astype(BF16)


def attend_self(query_ref, fresh_ref, cached, length_ref, out_ref):
    request_count, _, cache_length, _ = cached.shape
    row_count, width = query_ref.shape
    step_count = row_count // request_count
    key_count = request_count * cache_length
    row_request = lax.broadcasted_iota(jnp.int32, (row_count, key_count), 0) // step_count
    key_index = lax.broadcasted_iota(jnp.int32, (1, key_count), 1)
    limit = jnp.zeros((1, key_count), jnp.int32)
    for request in range(request_count):
        limit = jnp.where(key_index // cache_length == request, length_ref[request], limit)
    key_request = jnp.where(key_index % cache_length < limit, key_index // cache_length, -1)
    live = row_request == key_request
    fresh_row = lax.broadcasted_iota(jnp.int32, (row_count, row_count), 0)
    fresh_key = lax.broadcasted_iota(jnp.int32, (row_count, row_count), 1)
    fresh_live = (fresh_row // step_count == fresh_key // step_count) & (fresh_key <= fresh_row)
    scale = HDIM ** (-0.5)
    last = (((1,), (1,)), ((), ()))
    for head in range(width // HDIM):
        lanes = slice(head * HDIM, (head + 1) * HDIM)
        query = query_ref[:, lanes]
        keys = cached[:, 0, :, lanes].reshape(key_count, HDIM)
        values = cached[:, 1, :, lanes].reshape(key_count, HDIM)
        scores = lax.dot_general(query, keys, last, preferred_element_type=F32) * scale
        scores = jnp.where(live, scores, masked_value)
        fresh = lax.dot_general(query, fresh_ref[0, :, lanes], last, preferred_element_type=F32) * scale
        fresh = jnp.where(fresh_live, fresh, masked_value)
        top = jnp.maximum(
            jnp.max(scores, axis=1, keepdims=True), jnp.max(fresh, axis=1, keepdims=True)
        )
        weights = jnp.exp(scores - top)
        fresh_weights = jnp.exp(fresh - top)
        denom = jnp.sum(weights, axis=1, keepdims=True) + jnp.sum(fresh_weights, axis=1, keepdims=True)
        summed = jnp.dot(weights.astype(BF16), values, preferred_element_type=F32)
        summed = summed + jnp.dot(
            fresh_weights.astype(BF16), fresh_ref[1, :, lanes], preferred_element_type=F32
        )
        out_ref[:, lanes] = (summed / denom).astype(BF16)


def attend_blocks(messages, blocks):
    source_count, message_rows, _ = messages.shape
    head_count = message_rows // 8
    block_count, _, token_count, _ = blocks.shape
    rows = source_count * 8
    scale = HDIM ** (-0.5)
    values = messages.astype(F32)
    in_tile = lax.broadcasted_iota(jnp.int32, (source_count, 8, HDIM), 1)
    lane = lax.broadcasted_iota(jnp.int32, (source_count, 8, HDIM), 2)
    tags = jnp.where(in_tile < 3, values[:, 6:7, :], values[:, 7:8, :]).reshape(rows, HDIM)
    mine = [tags == F32(index + 1) for index in range(block_count)]
    parts = []
    for head in range(head_count):
        lanes = slice(head * HDIM, (head + 1) * HDIM)
        query = values[:, head * 8 : head * 8 + 8, :].reshape(rows, HDIM).astype(BF16)
        keys = blocks[:, 0, :, lanes].reshape(block_count * token_count, HDIM)
        scores = lax.dot_general(
            query, keys, (((1,), (1,)), ((), ())), preferred_element_type=F32
        )
        chosen = jnp.zeros((rows, token_count), F32)
        for index in range(block_count):
            chosen = jnp.where(
                mine[index], scores[:, index * token_count : (index + 1) * token_count], chosen
            )
        chosen = chosen * scale
        top = jnp.max(chosen, axis=1, keepdims=True)
        weights = jnp.exp(chosen - top)
        denom = jnp.sum(weights, axis=1, keepdims=True)
        spread = jnp.concatenate(
            [jnp.where(mine[index], weights, 0.0).astype(BF16) for index in range(block_count)], axis=1
        )
        held = blocks[:, 1, :, lanes].reshape(block_count * token_count, HDIM)
        summed = jnp.dot(spread, held, preferred_element_type=F32) / denom
        level = jnp.broadcast_to(top + jnp.log(denom), (rows, HDIM)).reshape(source_count, 8, HDIM)
        level = jnp.sum(jnp.where(lane % 8 == in_tile, level, 0.0), axis=1, keepdims=True)
        high = level.astype(BF16).astype(F32)
        middle = (level - high).astype(BF16).astype(F32)
        low = level - high - middle
        terms = jnp.where(lane < 8, high, jnp.where(lane < 16, middle, low))
        parts.append(jnp.where(in_tile == 6, terms, summed.reshape(source_count, 8, HDIM)))
    return jnp.concatenate(parts, axis=1).astype(BF16)


def row_levels(values):
    source_count, message_rows, _ = values.shape
    tiles = values.reshape(source_count * message_rows // 8, 8, HDIM)
    in_tile = lax.broadcasted_iota(jnp.int32, tiles.shape, 1)
    lane = lax.broadcasted_iota(jnp.int32, tiles.shape, 2)
    terms = jnp.broadcast_to(tiles[:, 6:7, :], tiles.shape)
    picked = jnp.where((lane < 24) & (lane % 8 == in_tile), terms, 0.0)
    levels = jnp.sum(picked, axis=2, keepdims=True)
    return jnp.broadcast_to(levels, tiles.shape).reshape(values.shape)


def main_kernel(
    shard_ref, rank_ref, position_ref, length_ref,
    send_ref, query_ref, fresh_ref, cache_ref, corpus_ref, weight_ref,
    self_ref, out_ref,
    cached, blocks, arrived, reply, returned, sums, levels,
    heads, gathered, weights, totals, out_send, out_recv,
    local_sem, query_send, query_recv, reply_send, reply_recv,
    x_send, x_recv, ring_send, ring_recv, head_send, head_recv,
    y_send, y_recv, core_send, core_recv, out_send_sem, out_recv_sem,
):
    shard_count, message_rows, _ = send_ref.shape
    x_count, y_count = GRID_OF[shard_count]
    layer = y_count * CORES
    tensor_count = gathered.shape[1]
    request_count = shard_ref.shape[0]
    me, mine = lax.axis_index("corpus"), lax.axis_index("tensor")
    x = me // layer
    y = (me // CORES) % y_count
    core = me % CORES

    def device_at(dx, dy, dc):
        return (((x + dx) % x_count) * y_count + (y + dy) % y_count) * CORES + (core + dc) % CORES

    def remote(source, target, send_sem, recv_sem, corpus=None, tensor=None):
        return pltpu.make_async_remote_copy(
            src_ref=source,
            dst_ref=target,
            send_sem=send_sem,
            recv_sem=recv_sem,
            device_id=(me if corpus is None else corpus, mine if tensor is None else tensor),
            device_id_type=MESH,
        )

    def wait_bytes(ref, sem):
        pltpu.make_async_copy(ref, ref, sem).wait()

    barrier = pltpu.get_barrier_semaphore()

    def greet_corpus(step, carry):
        pl.semaphore_signal(
            barrier, inc=1, device_id=((me + step) % shard_count, mine), device_id_type=MESH
        )
        return carry

    def greet_tensor(step, carry):
        pl.semaphore_signal(
            barrier, inc=1, device_id=(me, (mine + step) % tensor_count), device_id_type=MESH
        )
        return carry

    lax.fori_loop(1, shard_count, greet_corpus, 0)
    lax.fori_loop(1, tensor_count, greet_tensor, 0)
    cache_copy = pltpu.make_async_copy(cache_ref, cached, local_sem.at[0])
    corpus_copy = pltpu.make_async_copy(corpus_ref, blocks, local_sem.at[1])
    cache_copy.start()
    corpus_copy.start()
    columns = pl.ds(pl.multiple_of(x * HDIM, HDIM), HDIM)
    own_weight = pltpu.make_async_copy(weight_ref, weights.at[mine, :, columns], local_sem.at[2])
    own_weight.start()
    own_query = pltpu.make_async_copy(send_ref.at[me], arrived.at[me], query_recv.at[0])
    own_query.start()
    pl.semaphore_wait(barrier, shard_count - 1 + tensor_count - 1)

    def send_query(step, carry):
        target = device_at(step // layer, (step % layer) // CORES, step % CORES)
        remote(
            send_ref.at[target], arrived.at[me], query_send, query_recv.at[step // layer], target
        ).start()
        return carry

    lax.fori_loop(1, shard_count, send_query, 0)
    for dx in range(1, x_count):
        remote(
            weight_ref, weights.at[mine, :, columns], x_send, x_recv, device_at(dx, 0, 0)
        ).start()

    def ring_up(step):
        owner = (mine - step + tensor_count) % tensor_count
        return remote(
            weights.at[owner], weights.at[owner], ring_send.at[0, step], ring_recv.at[0, step],
            tensor=(mine + 1) % tensor_count,
        )

    def ring_down(step):
        owner = (mine + step) % tensor_count
        return remote(
            weights.at[owner], weights.at[owner], ring_send.at[1, step], ring_recv.at[1, step],
            tensor=(mine + tensor_count - 1) % tensor_count,
        )

    ups, downs = tensor_count // 2, (tensor_count - 1) // 2

    def ring_wait(step):
        if 0 <= step < ups:
            ring_up(step).wait_recv()
        if 0 <= step < downs:
            ring_down(step).wait_recv()

    def ring_step(step):
        ring_wait(step - 1)
        if step < ups:
            ring_up(step).start()
        if step < downs:
            ring_down(step).start()

    cache_copy.wait()
    attend_self(query_ref, fresh_ref, cached, length_ref, self_ref)

    own_weight.wait()
    x_wait = weights.at[mine, :, pl.ds(0, (x_count - 1) * HDIM)]
    wait_bytes(x_wait, x_recv)
    ring_step(0)

    corpus_copy.wait()

    def serve(dx, carry):
        first = pl.multiple_of(((x - dx + x_count) % x_count) * layer, layer)
        chunk = pl.ds(first, layer)
        wait_bytes(arrived.at[chunk], query_recv.at[dx])
        reply[chunk] = attend_blocks(arrived[chunk], blocks)

        def answer(step, inner):
            target = device_at(x_count - dx, step // CORES, step % CORES)
            remote(
                reply.at[target], returned.at[me], reply_send, reply_recv.at[dx], target
            ).start()
            return inner

        lax.fori_loop(jnp.where(dx == 0, 1, 0), layer, answer, 0)
        return carry

    lax.fori_loop(0, x_count, serve, 0)
    own_reply = pltpu.make_async_copy(reply.at[me], returned.at[me], reply_recv.at[0])
    own_reply.start()
    ring_step(1)

    def decode(dx, carry):
        first = pl.multiple_of(((x + dx) % x_count) * layer, layer)
        chunk = pl.ds(first, layer)
        wait_bytes(returned.at[chunk], reply_recv.at[dx])
        values = returned[chunk].astype(F32)
        sums[chunk] = values
        levels[chunk] = row_levels(values)
        return carry

    lax.fori_loop(0, x_count, decode, 0)

    tile_row = lax.broadcasted_iota(jnp.int32, (message_rows, HDIM), 0) % 8

    def combined(request):
        boundary = SPAN - position_ref[request] % SPAN
        late = tile_row >= boundary

        def item(ref, number):
            tile = ref[shard_ref[request, number]]
            second = rank_ref[request, number] == 1
            if number < NBR:
                return jnp.where(second, pltpu.roll(tile, message_rows - 3, 0), tile)
            return jnp.where(
                second, pltpu.roll(tile, message_rows - 2, 0), pltpu.roll(tile, 1, 0)
            )

        def pair(ref):
            return [
                jnp.where(late, item(ref, NBR + number), item(ref, number)) for number in range(NBR)
            ]

        held, level = pair(sums), pair(levels)
        joint = jnp.maximum(level[0], level[1])
        factors = [jnp.exp(entry - joint) for entry in level]
        return (factors[0] * held[0] + factors[1] * held[1]) / (factors[0] + factors[1])

    def combine(owner, carry):
        first = combined(owner * 2)
        second = pltpu.roll(combined(owner * 2 + 1), 4, 0)
        both = jnp.where(tile_row < 4, first, second)
        upper = jnp.concatenate([both[0:8], both[8:16]], axis=1)
        lower = jnp.concatenate([both[16:24], both[24:32]], axis=1)
        heads[owner] = jnp.concatenate([upper, lower], axis=0).astype(BF16)
        return carry

    lax.fori_loop(0, tensor_count, combine, 0)

    place = y * CORES + core
    own_heads = pltpu.make_async_copy(heads.at[mine], gathered.at[place, mine], head_recv)
    own_heads.start()

    def send_heads(step, carry):
        owner = (mine + step) % tensor_count
        remote(
            heads.at[owner], gathered.at[place, mine], head_send, head_recv, tensor=owner
        ).start()
        return carry

    lax.fori_loop(1, tensor_count, send_heads, 0)
    ring_step(2)
    wait_bytes(gathered.at[place], head_recv)

    def send_y(step, carry):
        remote(
            gathered.at[place], gathered.at[place], y_send, y_recv.at[step], device_at(0, step, 0)
        ).start()
        return carry

    def pass_core(index):
        return remote(
            gathered.at[index], gathered.at[index], core_send, core_recv, device_at(0, 0, 1)
        )

    lax.fori_loop(1, y_count, send_y, 0)
    pass_core(place).start()
    ring_step(3)

    def forward(step, carry):
        index = ((y - step + y_count) % y_count) * CORES + core
        wait_bytes(gathered.at[index], y_recv.at[step])
        pass_core(index).start()
        return carry

    lax.fori_loop(1, y_count, forward, 0)
    ring_wait(3)
    wait_bytes(gathered.at[pl.ds(0, y_count)], core_recv)

    half = gathered.shape[2] // 2
    rows = layer * half

    def project(owner):
        block = gathered[:, owner].astype(F32)
        left = jnp.concatenate(
            [block[:, :half].reshape(rows, -1), block[:, half:].reshape(rows, -1)], axis=1
        ).astype(BF16)
        return jnp.dot(left, weights[owner], preferred_element_type=F32)

    totals[...] = jnp.zeros_like(totals)

    def accumulate(owner, carry):
        product = project(owner)
        for dx in range(x_count):
            totals[dx * rows : (dx + 1) * rows, :] += product[:, dx * HDIM : (dx + 1) * HDIM]
        return carry

    lax.fori_loop(0, tensor_count, accumulate, 0)
    for row in range(half):
        for index in range(x_count):
            picked = totals[pl.ds(index * rows + row, layer, stride=half), :]
            out_send[index, row] = picked.astype(BF16)
    own_out = pltpu.make_async_copy(out_send.at[x], out_recv.at[x], out_recv_sem)
    own_out.start()
    for dx in range(1, x_count):
        remote(
            out_send.at[(x + dx) % x_count], out_recv.at[x], out_send_sem, out_recv_sem,
            device_at(dx, 0, 0),
        ).start()
    wait_bytes(out_recv, out_recv_sem)
    for index in range(x_count):
        out_ref[:, index * layer : (index + 1) * layer, :] = out_recv[index]

    wait_bytes(send_ref.at[pl.ds(0, shard_count - 1)], query_send)
    wait_bytes(reply.at[pl.ds(0, shard_count - 1)], reply_send)
    wait_bytes(x_wait, x_send)
    for step in range(ups):
        ring_up(step).wait_send()
    for step in range(downs):
        ring_down(step).wait_send()
    wait_bytes(heads.at[pl.ds(0, tensor_count - 1)], head_send)
    wait_bytes(gathered.at[pl.ds(0, y_count - 1)], y_send)
    wait_bytes(gathered.at[pl.ds(0, y_count)], core_send)
    wait_bytes(out_send.at[pl.ds(0, x_count - 1)], out_send_sem)


def on_device(
    self_query,
    cross_query,
    cache,
    step_kv,
    kv_length,
    positions,
    corpus_kv,
    neighbour_shard,
    neighbour_slot,
    out_weight,
):
    request_count, step_count, width = cross_query.shape
    head_count = width // HDIM
    shard_count = lax.axis_size("corpus")
    tensor_count = lax.axis_size("tensor")
    x_count, y_count = GRID_OF[shard_count]
    layer = y_count * CORES
    message_rows = head_count * 8
    row_count = request_count * step_count
    share = row_count // tensor_count
    smem = pl.BlockSpec(memory_space=pltpu.SMEM)
    vmem = pl.BlockSpec(memory_space=pltpu.VMEM)
    message = (shard_count, message_rows, HDIM)
    send, ranks = pl.pallas_call(
        pack_kernel,
        out_shape=(
            jax.ShapeDtypeStruct(message, BF16),
            jax.ShapeDtypeStruct(neighbour_shard.shape, jnp.int32),
        ),
        in_specs=[smem, smem, vmem],
        out_specs=(vmem, smem),
        scratch_shapes=[
            pltpu.VMEM((request_count, message_rows, HDIM), F32),
            pltpu.VMEM((4, request_count, message_rows, HDIM), F32),
            pltpu.VMEM(message, F32),
            pltpu.SMEM((shard_count,), jnp.int32),
        ],
        compiler_params=pltpu.CompilerParams(vmem_limit_bytes=32 * 1024 * 1024),
        name="pack_queries",
    )(neighbour_shard, neighbour_slot, cross_query)
    fresh = step_kv.transpose(1, 0, 2, 3).reshape(2, row_count, width)
    gather_shape = (layer, tensor_count, 2 * share, width // 2)
    out_shape = (share, shard_count, out_weight.shape[1])
    exchange = (x_count, share, layer, out_weight.shape[1])
    dma = pltpu.SemaphoreType.DMA
    self_heads, cross_out = pl.pallas_call(
        main_kernel,
        out_shape=(
            jax.ShapeDtypeStruct((row_count, width), BF16),
            jax.ShapeDtypeStruct(out_shape, BF16),
        ),
        in_specs=[smem] * 4 + [vmem] * 3 + [pl.BlockSpec(memory_space=pl.ANY)] * 2 + [vmem],
        out_specs=(vmem, vmem),
        scratch_shapes=[
            pltpu.VMEM(cache.shape, BF16),
            pltpu.VMEM(corpus_kv.shape, BF16),
            pltpu.VMEM(message, BF16),
            pltpu.VMEM(message, BF16),
            pltpu.VMEM(message, BF16),
            pltpu.VMEM(message, F32),
            pltpu.VMEM(message, F32),
            pltpu.VMEM(gather_shape[1:], BF16),
            pltpu.VMEM(gather_shape, BF16),
            pltpu.VMEM((tensor_count, width, x_count * HDIM), BF16),
            pltpu.VMEM((x_count * layer * share, HDIM), F32),
            pltpu.VMEM(exchange, BF16),
            pltpu.VMEM(exchange, BF16),
            dma((3,)),
            dma, dma((x_count,)),
            dma, dma((x_count,)),
            dma, dma,
            dma((2, max(1, tensor_count // 2))), dma((2, max(1, tensor_count // 2))),
            dma, dma,
            dma, dma((y_count,)),
            dma, dma,
            dma, dma,
        ],
        compiler_params=pltpu.CompilerParams(
            collective_id=0, has_side_effects=True, vmem_limit_bytes=56 * 1024 * 1024
        ),
        name="retrieve_and_project",
    )(
        neighbour_shard, ranks, positions, kv_length,
        send, self_query.reshape(row_count, width), fresh, cache, corpus_kv, out_weight,
    )
    return self_heads.reshape(request_count, step_count, width), cross_out


def solution(mesh):
    return jax.shard_map(
        on_device,
        mesh=mesh,
        in_specs=(
            P("corpus", None, "tensor"),
            P("corpus", None, "tensor"),
            P("corpus", None, None, "tensor"),
            P("corpus", None, None, "tensor"),
            P("corpus"),
            P("corpus"),
            P("corpus", None, None, "tensor"),
            P("corpus", None),
            P("corpus", None),
            P("tensor", "corpus"),
        ),
        out_specs=(P("corpus", None, "tensor"), P("tensor", None, "corpus")),
        check_vma=False,
    )
```

time: 285 us -> 104 us (0.36); the launches traced: 280 us -> 103 us
  waiting for transfers between devices: 166 us -> 0 us
  Pallas kernels: 0 us -> 92.2 us
  starting transfers between devices: 40.8 us -> 0 us
  local copies, waits for them, and re-layouts: 37.6 us -> 9.92 us
  matrix products: 16.2 us -> 0 us
  between operations: 14.5 us -> 0.66 us
  other arithmetic: 5.32 us -> 0 us
    pallas_call x0 -> x2, Pallas kernels: none -> 92.2 us  [the longest x1 89.5 us: on_device(): pl.pallas_call(main_kernel, out_shape=(jax.ShapeDtypeStruct((row_count, w...]
    all_gather x1 -> x0, waiting for transfers between devices: 84.9 us -> none  [on_device(): lax.all_gather(flat_heads[:, None, :], 'corpus', axis=1, tiled=True)]
    all_to_all x5 -> x0, waiting for transfers between devices: 47.8 us -> none  [the longest x1 25.7 us: on_device(): lax.all_to_all(partials[0], 'corpus', split_axis=0, concat_axis=0, tiled=...]
    all_to_all x5 -> x0, starting transfers between devices: 40.7 us -> none  [the longest x1 11.6 us: on_device(): lax.all_to_all(send_tags, 'corpus', split_axis=0, concat_axis=0, tiled=True)]
    reduce_scatter x1 -> x0, waiting for transfers between devices: 33 us -> none  [on_device(): lax.psum_scatter(partial_terms, 'tensor', scatter_dimension=0, tiled=True)]
    dot_general x21 -> x0, matrix products: 16.2 us -> none  [the longest x1 8.19 us: on_device(): jnp.einsum('rcw,wd->rcd', lax.all_gather(flat_heads[:, None, :], 'corpus'...]
    unnamed x47 -> x11, local copies, waits for them, and re-layouts: 14.4 us -> 5.3 us
    scatter x2 -> x0, local copies, waits for them, and re-layouts: 8.32 us -> none  [the longest x1 7.55 us: on_device(): send_queries = jnp.zeros((shard_count * slot_count, step_count, width), j...]
  transfers between devices with their start and end apart: 7 -> 0, of which waited for: 6 -> 0; matrix products, arithmetic and copies ran while one was open for 13% -> 0% of each run, Pallas kernels for 0% -> 0%
where the time goes in v1:
time: 104 us; the launch traced here: 103 us
  Pallas kernels  92.2 us (89%)
  local copies, waits for them, and re-layouts  9.92 us (10%)
    pallas_call x1, Pallas kernels, on_device(): pl.pallas_call(main_kernel, out_shape=(jax.ShapeDtypeStruct((row_count, w...  89.5 us
    unnamed x11, local copies, waits for them, and re-layouts  5.3 us
    pallas_call x1, Pallas kernels, on_device(): pl.pallas_call(pack_kernel, out_shape=(jax.ShapeDtypeStruct(message, BF16...  2.68 us

profile of v1, /device:TPU:1, one launch (start us, length us, event | category | flops | bytes accessed | tf_op | source)
XLA Modules:
  0.0 102.8 jit_solution(7953328118541440618)
XLA Ops:
  0.6 0.8 copy.15.shard_ref
  1.4 0.0 copy-start.1
  1.4 0.8 copy.13.slot_ref
  2.2 1.5 %reshape.13.query_ref = bf16[64,512]{1,0:T(8,128)(2,1)} reshape(bf16[16,4,512]{2,1,0:T(4,128)(2,1)} %param.10) | data formatting | bytes 131072 | tf_op jit(solution)/shard_map/reshape | solution.py:512
  3.6 0.9 copy.14
  4.6 0.7 reshape.14.fresh_ref
  5.3 0.0 copy-start.2
  5.3 0.8 copy-done.2
  6.1 2.7 %pack_queries.1 = (bf16[64,32,128]{2,1,0:T(8,128)(2,1)S(1)}, s32[16,4]{1,0:T(8,128)S(1)}) custom-call(s32[16,4]{1,0:T(8,128)S(1)} %copy.15.shard_ref, s32[16,4]{1,0:T(8,128)S(1)} %copy.13.slot_ref, bf16[16,4,512]{2,1,0:T(4,128)(2,1)S(1)} %copy-done.2), custom_call_target="tpu_custom_call" | custom-call | tf_op jit(solution)/shard_map/pack_queries/pallas_call | solution.py:452
  8.8 0.0 copy-start
  8.8 0.8 copy-done
  9.6 0.0 copy-start.3
  9.6 0.6 copy-done.3
  10.2 0.0 copy-done.1
  10.2 89.5 %retrieve_and_project.1 = (bf16[64,512]{1,0:T(8,128)(2,1)}, bf16[8,64,128]{2,1,0:T(8,128)(2,1)}) custom-call(s32[16,4]{1,0:T(8,128)} %copy-done.1, s32[16,4]{1,0:T(8,128)} %copy-done.3, s32[16]{0:T(128)} %position_ref.1, s32[16]{0:T(128)} %length_ref.1, bf16[64,32,128]{2,1,0:T(8,128)(2,1)} %copy-done, bf16[64,512]{1,0:T(8,128)(2,1)} %reshape.13.query_ref, ...), custom_call_target="tpu_custom_call" | custom-call | tf_op jit(solution)/shard_map/retrieve_and_project/pallas_call | solution.py:474
  99.7 1.5 %reshape.15 = bf16[16,4,512]{2,1,0:T(4,128)(2,1)} reshape(bf16[64,512]{1,0:T(8,128)(2,1)} %get-tuple-element.8) | data formatting | bytes 131072 | tf_op jit(solution)/shard_map/reshape | solution.py:514
  101.2 1.6 %copy.17 = bf16[8,64,128]{2,1,0:T(8,128)(2,1)} copy(bf16[8,64,128]{2,1,0:T(8,128)(2,1)} %get-tuple-element.13) | data formatting | bytes 262144
Async XLA Ops:
  1.4 8.8 %copy-start.1 = (s32[16,4]{1,0:T(8,128)}, s32[16,4]{1,0:T(8,128)S(1)}, u32[]{:S(2)}) copy-start(s32[16,4]{1,0:T(8,128)S(1)} %copy.15.shard_ref) | copy-start | bytes 772
  5.3 0.8 copy-start.2
  8.8 0.8 copy-start
  9.6 0.6 copy-start.3

commit v2 on v1

--- a/solution.py
+++ b/solution.py
@@ -18,51 +18,52 @@
 BF16 = jnp.bfloat16
 
 
-def pack_kernel(shard_ref, slot_ref, query_ref, send_ref, rank_ref, base, variants, total, counts):
-    request_count, step_count, _ = query_ref.shape
+def pack_queries(shards, slots, query, steps, columns, ranks, total, send_ref):
+    item_count, request_count = shards.shape
     shard_count, message_rows, _ = send_ref.shape
     head_count = message_rows // 8
-    base[...] = jnp.zeros_like(base)
-    queries = query_ref[...].astype(F32)
-    for head in range(head_count):
-        base[:, head * 8 : head * 8 + step_count, :] = queries[:, :, head * HDIM : (head + 1) * HDIM]
-    flat = base[...].reshape(request_count * message_rows, HDIM)
-    row = lax.broadcasted_iota(jnp.int32, flat.shape, 0) % 8
-    size = flat.shape[0]
-    moved = (
-        jnp.where(row < 3, flat, 0.0),
-        jnp.where((row >= 3) & (row < 6), pltpu.roll(flat, 3, 0), 0.0),
-        jnp.where(row < 3, pltpu.roll(flat, size - 1, 0), 0.0),
-        jnp.where((row >= 3) & (row < 6), pltpu.roll(flat, 2, 0), 0.0),
+    count = item_count * request_count
+    lane = lax.broadcasted_iota(jnp.int32, (1, HDIM), 1)
+    shard_row = jnp.full((1, HDIM), -1, jnp.int32)
+    tag_row = jnp.zeros((1, HDIM), jnp.int32)
+    for number in range(count):
+        item, request = divmod(number, request_count)
+        shard = shards[item, request]
+        shard_row = jnp.where(lane == number, shard, shard_row)
+        tag_row = jnp.where(lane == number, slots[item, request] + 1, tag_row)
+        columns[number : number + 1, :] = jnp.full((1, HDIM), shard, jnp.int32)
+    same = columns[...] == shard_row
+    here = lax.broadcasted_iota(jnp.int32, same.shape, 0)
+    there = lax.broadcasted_iota(jnp.int32, same.shape, 1)
+    ranks[...] = jnp.broadcast_to(
+        jnp.sum(jnp.where(same & (there < here), 1.0, 0.0), axis=1, keepdims=True), same.shape
     )
-    for number, values in enumerate(moved):
-        variants[number] = values.reshape(request_count, message_rows, HDIM)
-    total[...] = jnp.zeros_like(total)
-
-    def clear(index, carry):
-        counts[index] = 0
-        return carry
-
-    lax.fori_loop(0, shard_count, clear, 0)
-    tile_row = lax.broadcasted_iota(jnp.int32, (message_rows, HDIM), 0) % 8
-
-    def place(request, carry):
-        for item in range(2 * NBR):
-            shard = shard_ref[request, item]
-            rank = counts[shard]
-            counts[shard] = rank + 1
-            rank_ref[request, item] = rank
-            number = rank + (2 if item >= NBR else 0)
-            tag = (slot_ref[request, item] + 1).astype(F32)
-            tile = jnp.where(tile_row == rank + 6, tag, variants[number, request])
-            total[shard] = total[shard] + tile
-        return carry
-
-    lax.fori_loop(0, request_count, place, 0)
-    send_ref[...] = total[...].astype(BF16)
-
-
-def attend_self(query_ref, fresh_ref, cached, length_ref, out_ref):
+    rank_row = jnp.sum(jnp.where(same & (here < there), 1.0, 0.0), axis=0, keepdims=True)
+    for request in range(request_count):
+        rows = query[request].astype(F32)
+        for step in range(rows.shape[0]):
+            steps[step, request : request + 1, :] = rows[step : step + 1, :]
+    at_shard = shard_row == lax.broadcasted_iota(jnp.int32, (shard_count, HDIM), 0)
+    for rank in range(2):
+        chosen = jnp.where(at_shard & (rank_row == rank), 1.0, 0.0)
+        tag = jnp.sum(chosen * tag_row.astype(F32), axis=1, keepdims=True)
+        tag = jnp.broadcast_to(tag, (shard_count, HDIM))
+        for head in range(head_count):
+            total[pl.ds(head * 8 + 6 + rank, shard_count, stride=message_rows), :] = tag
+        picker = chosen[:, :count].astype(BF16)
+        for row in range(3):
+            early, late = steps[row], steps[row + 1]
+            items = jnp.concatenate([early] * NBR + [late] * NBR, axis=0).astype(BF16)
+            packed = jnp.dot(picker, items, preferred_element_type=F32)
+            for head in range(head_count):
+                start = head * 8 + rank * 3 + row
+                total[pl.ds(start, shard_count, stride=message_rows), :] = packed[
+                    :, head * HDIM : (head + 1) * HDIM
+                ]
+    send_ref[...] = total[...].reshape(send_ref.shape).astype(BF16)
+
+
+def attend_self(query_ref, fresh_ref, cached, length_ref, out_ref, heads):
     request_count, _, cache_length, _ = cached.shape
     row_count, width = query_ref.shape
     step_count = row_count // request_count
@@ -79,14 +80,14 @@
     fresh_live = (fresh_row // step_count == fresh_key // step_count) & (fresh_key <= fresh_row)
     scale = HDIM ** (-0.5)
     last = (((1,), (1,)), ((), ()))
-    for head in range(width // HDIM):
+    for head in heads:
         lanes = slice(head * HDIM, (head + 1) * HDIM)
-        query = query_ref[:, lanes]
+        query = query_ref[:, lanes].astype(BF16)
         keys = cached[:, 0, :, lanes].reshape(key_count, HDIM)
         values = cached[:, 1, :, lanes].reshape(key_count, HDIM)
         scores = lax.dot_general(query, keys, last, preferred_element_type=F32) * scale
         scores = jnp.where(live, scores, masked_value)
-        fresh = lax.dot_general(query, fresh_ref[0, :, lanes], last, preferred_element_type=F32) * scale
+        fresh = lax.dot_general(query, fresh_ref[0, :, lanes].astype(BF16), last, preferred_element_type=F32) * scale
         fresh = jnp.where(fresh_live, fresh, masked_value)
         top = jnp.maximum(
             jnp.max(scores, axis=1, keepdims=True), jnp.max(fresh, axis=1, keepdims=True)
@@ -96,9 +97,12 @@
         denom = jnp.sum(weights, axis=1, keepdims=True) + jnp.sum(fresh_weights, axis=1, keepdims=True)
         summed = jnp.dot(weights.astype(BF16), values, preferred_element_type=F32)
         summed = summed + jnp.dot(
-            fresh_weights.astype(BF16), fresh_ref[1, :, lanes], preferred_element_type=F32
-        )
-        out_ref[:, lanes] = (summed / denom).astype(BF16)
+            fresh_weights.astype(BF16), fresh_ref[1, :, lanes].astype(BF16), preferred_element_type=F32
+        )
+        result = summed / denom
+        for request in range(request_count):
+            rows = result[request * step_count : (request + 1) * step_count, :]
+            out_ref[request, :, lanes] = rows.astype(BF16)
 
 
 def attend_blocks(messages, blocks):
@@ -156,20 +160,21 @@
 
 
 def main_kernel(
-    shard_ref, rank_ref, position_ref, length_ref,
-    send_ref, query_ref, fresh_ref, cache_ref, corpus_ref, weight_ref,
+    shard_ref, slot_ref, position_ref, length_ref,
+    cross_ref, query_ref, fresh_ref, cache_ref, corpus_ref, weight_ref,
     self_ref, out_ref,
-    cached, blocks, arrived, reply, returned, sums, levels,
+    shards, slots, cross, query, fresh, query_rows, fresh_rows, steps, columns, ranks, packed,
+    cached, blocks, send, arrived, reply, returned, sums, levels,
     heads, gathered, weights, totals, out_send, out_recv,
-    local_sem, query_send, query_recv, reply_send, reply_recv,
+    entered, local_sem, query_send, query_recv, reply_send, reply_recv,
     x_send, x_recv, ring_send, ring_recv, head_send, head_recv,
     y_send, y_recv, core_send, core_recv, out_send_sem, out_recv_sem,
 ):
-    shard_count, message_rows, _ = send_ref.shape
+    shard_count, message_rows, _ = send.shape
     x_count, y_count = GRID_OF[shard_count]
     layer = y_count * CORES
     tensor_count = gathered.shape[1]
-    request_count = shard_ref.shape[0]
+    request_count, step_count, _ = cross.shape
     me, mine = lax.axis_index("corpus"), lax.axis_index("tensor")
     x = me // layer
     y = (me // CORES) % y_count
@@ -191,83 +196,106 @@
     def wait_bytes(ref, sem):
         pltpu.make_async_copy(ref, ref, sem).wait()
 
+    small = [
+        pltpu.make_async_copy(source, target, local_sem.at[index])
+        for index, (source, target) in enumerate(
+            [(shard_ref, shards), (slot_ref, slots), (cross_ref, cross), (query_ref, query),
+             (fresh_ref, fresh)]
+        )
+    ]
+    for copy in small:
+        copy.start()
+
     barrier = pltpu.get_barrier_semaphore()
 
-    def greet_corpus(step, carry):
-        pl.semaphore_signal(
-            barrier, inc=1, device_id=((me + step) % shard_count, mine), device_id_type=MESH
-        )
+    def greet(sem, corpus, tensor):
+        pl.semaphore_signal(sem, inc=1, device_id=(corpus, tensor), device_id_type=MESH)
+
+    for dx in range(1, x_count):
+        greet(barrier, device_at(dx, 0, 0), mine)
+
+    def greet_layer(step, carry):
+        greet(barrier, device_at(0, step // CORES, step % CORES), mine)
         return carry
 
     def greet_tensor(step, carry):
-        pl.semaphore_signal(
-            barrier, inc=1, device_id=(me, (mine + step) % tensor_count), device_id_type=MESH
-        )
-        return carry
-
-    lax.fori_loop(1, shard_count, greet_corpus, 0)
+        greet(barrier, me, (mine + step) % tensor_count)
+        return carry
+
+    lax.fori_loop(1, layer, greet_layer, 0)
     lax.fori_loop(1, tensor_count, greet_tensor, 0)
-    cache_copy = pltpu.make_async_copy(cache_ref, cached, local_sem.at[0])
-    corpus_copy = pltpu.make_async_copy(corpus_ref, blocks, local_sem.at[1])
+    own_weight = pltpu.make_async_copy(weight_ref, weights.at[mine, x], local_sem.at[5])
+    own_weight.start()
+    cache_copy = pltpu.make_async_copy(cache_ref, cached, local_sem.at[6])
+    corpus_copy = pltpu.make_async_copy(corpus_ref, blocks, local_sem.at[7])
     cache_copy.start()
     corpus_copy.start()
-    columns = pl.ds(pl.multiple_of(x * HDIM, HDIM), HDIM)
-    own_weight = pltpu.make_async_copy(weight_ref, weights.at[mine, :, columns], local_sem.at[2])
-    own_weight.start()
-    own_query = pltpu.make_async_copy(send_ref.at[me], arrived.at[me], query_recv.at[0])
+    for copy in small:
+        copy.wait()
+    pack_queries(shards, slots, cross, steps, columns, ranks, packed, send)
+    own_query = pltpu.make_async_copy(send.at[me], arrived.at[me], query_recv.at[0])
     own_query.start()
-    pl.semaphore_wait(barrier, shard_count - 1 + tensor_count - 1)
-
-    def send_query(step, carry):
-        target = device_at(step // layer, (step % layer) // CORES, step % CORES)
-        remote(
-            send_ref.at[target], arrived.at[me], query_send, query_recv.at[step // layer], target
-        ).start()
-        return carry
-
-    lax.fori_loop(1, shard_count, send_query, 0)
+    pl.semaphore_wait(barrier, x_count - 1 + layer - 1 + tensor_count - 1)
+    for dx in range(1, x_count):
+        greet(entered, device_at(dx, 0, 0), mine)
+    own_weight.wait()
+
     for dx in range(1, x_count):
         remote(
-            weight_ref, weights.at[mine, :, columns], x_send, x_recv, device_at(dx, 0, 0)
+            weight_ref, weights.at[mine, x], x_send, x_recv.at[dx], device_at(dx, 0, 0)
         ).start()
-
-    def ring_up(step):
-        owner = (mine - step + tensor_count) % tensor_count
+    ups, downs = tensor_count // 2, (tensor_count - 1) // 2
+
+    def ring_copy(down, step, offset):
+        owner = (mine + (step if down else tensor_count - step)) % tensor_count
+        piece = weights.at[owner, (x + offset) % x_count]
+        after = (mine + (tensor_count - 1 if down else 1)) % tensor_count
         return remote(
-            weights.at[owner], weights.at[owner], ring_send.at[0, step], ring_recv.at[0, step],
-            tensor=(mine + 1) % tensor_count,
-        )
-
-    def ring_down(step):
-        owner = (mine + step) % tensor_count
-        return remote(
-            weights.at[owner], weights.at[owner], ring_send.at[1, step], ring_recv.at[1, step],
-            tensor=(mine + tensor_count - 1) % tensor_count,
-        )
-
-    ups, downs = tensor_count // 2, (tensor_count - 1) // 2
-
-    def ring_wait(step):
+            piece, piece, ring_send.at[down, step, offset], ring_recv.at[down, step, offset],
+            tensor=after,
+        )
+
+    def ring_wait(step, offset):
         if 0 <= step < ups:
-            ring_up(step).wait_recv()
+            ring_copy(0, step, offset).wait_recv()
         if 0 <= step < downs:
-            ring_down(step).wait_recv()
-
-    def ring_step(step):
-        ring_wait(step - 1)
+            ring_copy(1, step, offset).wait_recv()
+
+    def ring_step(step, offset):
+        ring_wait(step - 1, offset)
         if step < ups:
-            ring_up(step).start()
+            ring_copy(0, step, offset).start()
         if step < downs:
-            ring_down(step).start()
-
+            ring_copy(1, step, offset).start()
+
+    ring_step(0, 0)
+    pl.semaphore_wait(entered, x_count - 1)
+
+    def send_queries(dx, first):
+        def body(step, carry):
+            target = device_at(dx, step // CORES, step % CORES)
+            remote(
+                send.at[target], arrived.at[me], query_send, query_recv.at[dx], target
+            ).start()
+            return carry
+
+        lax.fori_loop(first, layer, body, 0)
+
+    for dx in range(x_count):
+        send_queries(dx, 1 if dx == 0 else 0)
+
+    for request in range(request_count):
+        rows = slice(request * step_count, (request + 1) * step_count)
+        query_rows[rows, :] = query[request].astype(F32)
+        for index in range(2):
+            fresh_rows[index, rows, :] = fresh[request, index].astype(F32)
     cache_copy.wait()
-    attend_self(query_ref, fresh_ref, cached, length_ref, self_ref)
-
-    own_weight.wait()
-    x_wait = weights.at[mine, :, pl.ds(0, (x_count - 1) * HDIM)]
-    wait_bytes(x_wait, x_recv)
-    ring_step(0)
-
+    all_heads = range(message_rows // 8)
+    attend_self(query_rows, fresh_rows, cached, length_ref, self_ref, all_heads[:2])
+    for offset in range(1, x_count):
+        wait_bytes(weights.at[mine, (x + offset) % x_count], x_recv.at[x_count - offset])
+        ring_step(0, offset)
+    attend_self(query_rows, fresh_rows, cached, length_ref, self_ref, all_heads[2:])
     corpus_copy.wait()
 
     def serve(dx, carry):
@@ -284,12 +312,12 @@
             return inner
 
         lax.fori_loop(jnp.where(dx == 0, 1, 0), layer, answer, 0)
+        ring_step(1, dx)
         return carry
 
     lax.fori_loop(0, x_count, serve, 0)
     own_reply = pltpu.make_async_copy(reply.at[me], returned.at[me], reply_recv.at[0])
     own_reply.start()
-    ring_step(1)
 
     def decode(dx, carry):
         first = pl.multiple_of(((x + dx) % x_count) * layer, layer)
@@ -298,6 +326,7 @@
         values = returned[chunk].astype(F32)
         sums[chunk] = values
         levels[chunk] = row_levels(values)
+        ring_step(2, dx)
         return carry
 
     lax.fori_loop(0, x_count, decode, 0)
@@ -309,8 +338,8 @@
         late = tile_row >= boundary
 
         def item(ref, number):
-            tile = ref[shard_ref[request, number]]
-            second = rank_ref[request, number] == 1
+            tile = ref[shards[number, request]]
+            second = ranks[pl.ds(number * request_count + request, 1), :] == 1.0
             if number < NBR:
                 return jnp.where(second, pltpu.roll(tile, message_rows - 3, 0), tile)
             return jnp.where(
@@ -350,32 +379,66 @@
         return carry
 
     lax.fori_loop(1, tensor_count, send_heads, 0)
-    ring_step(2)
+    ring_step(3, 0)
     wait_bytes(gathered.at[place], head_recv)
 
-    def send_y(step, carry):
+    def slot_at(dy):
+        return ((y + dy) % y_count) * CORES + core
+
+    def send_y(ref, dy, number):
+        return remote(ref, ref, y_send.at[number], y_recv.at[number], device_at(0, dy, 0))
+
+    def pass_core(index):
         remote(
-            gathered.at[place], gathered.at[place], y_send, y_recv.at[step], device_at(0, step, 0)
+            gathered.at[index], gathered.at[index], core_send, core_recv, device_at(0, 0, 1)
         ).start()
-        return carry
-
-    def pass_core(index):
-        return remote(
-            gathered.at[index], gathered.at[index], core_send, core_recv, device_at(0, 0, 1)
-        )
-
-    lax.fori_loop(1, y_count, send_y, 0)
-    pass_core(place).start()
-    ring_step(3)
-
-    def forward(step, carry):
-        index = ((y - step + y_count) % y_count) * CORES + core
-        wait_bytes(gathered.at[index], y_recv.at[step])
-        pass_core(index).start()
-        return carry
-
-    lax.fori_loop(1, y_count, forward, 0)
-    ring_wait(3)
+
+    own = gathered.at[place]
+    if y_count == 8:
+        halves = (pl.ds(0, tensor_count // 2), pl.ds(tensor_count // 2, tensor_count // 2))
+        far_low, far_high = (gathered.at[slot_at(4), half] for half in halves)
+        first = [send_y(own, 2, 1), send_y(own, -2 + y_count, 3), send_y(own, 1, 0),
+                 send_y(own, y_count - 1, 2)]
+        for copy in first:
+            copy.start()
+        pass_core(place)
+        ring_step(3, 1)
+        below, above = gathered.at[slot_at(y_count - 2)], gathered.at[slot_at(2)]
+        wait_bytes(below, y_recv.at[1])
+        second = [send_y(gathered.at[slot_at(y_count - 2), halves[0]], 2, 6), send_y(below, 1, 4)]
+        for copy in second:
+            copy.start()
+        wait_bytes(above, y_recv.at[3])
+        third = [send_y(gathered.at[slot_at(2), halves[1]], y_count - 2, 7),
+                 send_y(above, y_count - 1, 5)]
+        for copy in third:
+            copy.start()
+        pass_core(slot_at(y_count - 2))
+        pass_core(slot_at(2))
+        for dy, number in ((y_count - 1, 0), (1, 2)):
+            wait_bytes(gathered.at[slot_at(dy)], y_recv.at[number])
+            pass_core(slot_at(dy))
+        ring_step(3, 2)
+        ring_step(3, 3)
+        for dy, number in ((y_count - 3, 4), (3, 5)):
+            wait_bytes(gathered.at[slot_at(dy)], y_recv.at[number])
+            pass_core(slot_at(dy))
+        wait_bytes(far_low, y_recv.at[6])
+        wait_bytes(far_high, y_recv.at[7])
+        pass_core(slot_at(4))
+        y_copies = first + second + third
+    else:
+        y_copies = [send_y(own, dy, dy) for dy in range(1, y_count)]
+        for copy in y_copies:
+            copy.start()
+        pass_core(place)
+        for dy in range(1, y_count):
+            wait_bytes(gathered.at[slot_at(y_count - dy)], y_recv.at[dy])
+            pass_core(slot_at(y_count - dy))
+        for offset in range(1, x_count):
+            ring_step(3, offset)
+    for offset in range(x_count):
+        ring_wait(3, offset)
     wait_bytes(gathered.at[pl.ds(0, y_count)], core_recv)
 
     half = gathered.shape[2] // 2
@@ -386,7 +449,8 @@
         left = jnp.concatenate(
             [block[:, :half].reshape(rows, -1), block[:, half:].reshape(rows, -1)], axis=1
         ).astype(BF16)
-        return jnp.dot(left, weights[owner], preferred_element_type=F32)
+        right = jnp.concatenate([weights[owner, index] for index in range(x_count)], axis=1)
+        return jnp.dot(left, right, preferred_element_type=F32)
 
     totals[...] = jnp.zeros_like(totals)
 
@@ -412,15 +476,16 @@
     for index in range(x_count):
         out_ref[:, index * layer : (index + 1) * layer, :] = out_recv[index]
 
-    wait_bytes(send_ref.at[pl.ds(0, shard_count - 1)], query_send)
+    wait_bytes(send.at[pl.ds(0, shard_count - 1)], query_send)
     wait_bytes(reply.at[pl.ds(0, shard_count - 1)], reply_send)
-    wait_bytes(x_wait, x_send)
-    for step in range(ups):
-        ring_up(step).wait_send()
-    for step in range(downs):
-        ring_down(step).wait_send()
+    wait_bytes(weights.at[mine, pl.ds(0, x_count - 1)], x_send)
+    for down, length in ((0, ups), (1, downs)):
+        for step in range(length):
+            for offset in range(x_count):
+                ring_copy(down, step, offset).wait_send()
     wait_bytes(heads.at[pl.ds(0, tensor_count - 1)], head_send)
-    wait_bytes(gathered.at[pl.ds(0, y_count - 1)], y_send)
+    for copy in y_copies:
+        copy.wait_send()
     wait_bytes(gathered.at[pl.ds(0, y_count)], core_send)
     wait_bytes(out_send.at[pl.ds(0, x_count - 1)], out_send_sem)
 
@@ -448,40 +513,36 @@
     share = row_count // tensor_count
     smem = pl.BlockSpec(memory_space=pltpu.SMEM)
     vmem = pl.BlockSpec(memory_space=pltpu.VMEM)
+    hbm = pl.BlockSpec(memory_space=pl.ANY)
     message = (shard_count, message_rows, HDIM)
-    send, ranks = pl.pallas_call(
-        pack_kernel,
-        out_shape=(
-            jax.ShapeDtypeStruct(message, BF16),
-            jax.ShapeDtypeStruct(neighbour_shard.shape, jnp.int32),
-        ),
-        in_specs=[smem, smem, vmem],
-        out_specs=(vmem, smem),
-        scratch_shapes=[
-            pltpu.VMEM((request_count, message_rows, HDIM), F32),
-            pltpu.VMEM((4, request_count, message_rows, HDIM), F32),
-            pltpu.VMEM(message, F32),
-            pltpu.SMEM((shard_count,), jnp.int32),
-        ],
-        compiler_params=pltpu.CompilerParams(vmem_limit_bytes=32 * 1024 * 1024),
-        name="pack_queries",
-    )(neighbour_shard, neighbour_slot, cross_query)
-    fresh = step_kv.transpose(1, 0, 2, 3).reshape(2, row_count, width)
     gather_shape = (layer, tensor_count, 2 * share, width // 2)
     out_shape = (share, shard_count, out_weight.shape[1])
     exchange = (x_count, share, layer, out_weight.shape[1])
     dma = pltpu.SemaphoreType.DMA
+    ring_shape = (2, max(1, tensor_count // 2), x_count)
     self_heads, cross_out = pl.pallas_call(
         main_kernel,
         out_shape=(
-            jax.ShapeDtypeStruct((row_count, width), BF16),
+            jax.ShapeDtypeStruct(self_query.shape, BF16),
             jax.ShapeDtypeStruct(out_shape, BF16),
         ),
-        in_specs=[smem] * 4 + [vmem] * 3 + [pl.BlockSpec(memory_space=pl.ANY)] * 2 + [vmem],
+        in_specs=[hbm] * 2 + [smem] * 2 + [hbm] * 6,
         out_specs=(vmem, vmem),
         scratch_shapes=[
+            pltpu.SMEM((2 * NBR, request_count), jnp.int32),
+            pltpu.SMEM((2 * NBR, request_count), jnp.int32),
+            pltpu.VMEM(cross_query.shape, BF16),
+            pltpu.VMEM(self_query.shape, BF16),
+            pltpu.VMEM(step_kv.shape, BF16),
+            pltpu.VMEM((row_count, width), F32),
+            pltpu.VMEM((2, row_count, width), F32),
+            pltpu.VMEM((step_count, request_count, width), F32),
+            pltpu.VMEM((2 * NBR * request_count, HDIM), jnp.int32),
+            pltpu.VMEM((2 * NBR * request_count, HDIM), F32),
+            pltpu.VMEM((shard_count * message_rows, HDIM), F32),
             pltpu.VMEM(cache.shape, BF16),
             pltpu.VMEM(corpus_kv.shape, BF16),
+            pltpu.VMEM(message, BF16),
             pltpu.VMEM(message, BF16),
             pltpu.VMEM(message, BF16),
             pltpu.VMEM(message, BF16),
@@ -489,17 +550,18 @@
             pltpu.VMEM(message, F32),
             pltpu.VMEM(gather_shape[1:], BF16),
             pltpu.VMEM(gather_shape, BF16),
-            pltpu.VMEM((tensor_count, width, x_count * HDIM), BF16),
+            pltpu.VMEM((tensor_count, x_count, width, HDIM), BF16),
             pltpu.VMEM((x_count * layer * share, HDIM), F32),
             pltpu.VMEM(exchange, BF16),
             pltpu.VMEM(exchange, BF16),
-            dma((3,)),
+            pltpu.SemaphoreType.REGULAR,
+            dma((8,)),
             dma, dma((x_count,)),
             dma, dma((x_count,)),
+            dma, dma((x_count,)),
+            dma(ring_shape), dma(ring_shape),
             dma, dma,
-            dma((2, max(1, tensor_count // 2))), dma((2, max(1, tensor_count // 2))),
-            dma, dma,
-            dma, dma((y_count,)),
+            dma((8,)), dma((8,)),
             dma, dma,
             dma, dma,
         ],
@@ -508,10 +570,10 @@
         ),
         name="retrieve_and_project",
     )(
-        neighbour_shard, ranks, positions, kv_length,
-        send, self_query.reshape(row_count, width), fresh, cache, corpus_kv, out_weight,
+        neighbour_shard.T, neighbour_slot.T, positions, kv_length,
+        cross_query, self_query, step_kv, cache, corpus_kv, out_weight,
     )
-    return self_heads.reshape(request_count, step_count, width), cross_out
+    return self_heads, cross_out
 
 
 def solution(mesh):

time: 104 us -> 83.6 us (0.80)
  Pallas kernels: 92.2 us -> 79.7 us
  local copies, waits for them, and re-layouts: 9.92 us -> 3.06 us
    pallas_call x2 -> x1, Pallas kernels: 92.2 us -> 79.7 us  [on_device(): pl.pallas_call(main_kernel, out_shape=(jax.ShapeDtypeStruct(self_query.sh...]
    reshape x3 -> x0, local copies, waits for them, and re-layouts: 3.67 us -> none  [the longest x1 1.49 us: on_device(): return (self_heads.reshape(request_count, step_count, width), cross_out)]
    unnamed x11 -> x2, local copies, waits for them, and re-layouts: 5.3 us -> 3.06 us
where the time goes in v2:
time: 83.6 us; the launch traced here: 83.4 us
  Pallas kernels  79.7 us (95%)
  local copies, waits for them, and re-layouts  3.06 us (4%)
    pallas_call x1, Pallas kernels, on_device(): pl.pallas_call(main_kernel, out_shape=(jax.ShapeDtypeStruct(self_query.sh...  79.7 us
    unnamed x2, local copies, waits for them, and re-layouts  3.06 us

profile of v2, /device:TPU:1, one launch (start us, length us, event | category | flops | bytes accessed | tf_op | source)
XLA Modules:
  0.0 83.4 jit_solution(7841623397167499706)
XLA Ops:
  0.6 79.7 %retrieve_and_project.1 = (bf16[16,4,512]{2,1,0:T(4,128)(2,1)}, bf16[8,64,128]{2,1,0:T(8,128)(2,1)}) custom-call(s32[4,16]{1,0:T(4,128)} %bitcast.2, s32[4,16]{1,0:T(4,128)} %bitcast.3, s32[16]{0:T(128)} %position_ref.1, s32[16]{0:T(128)} %length_ref.1, bf16[16,4,512]{2,1,0:T(4,128)(2,1)} %cross_ref.1, bf16[16,4,512]{2,1,0:T(4,128)(2,1)} %query_ref.1, ...), custom_call_target="tpu_custom_call" | custom-call | tf_op jit(solution)/shard_map/retrieve_and_project/pallas_call | solution.py:523
  80.3 1.5 %copy.14 = bf16[16,4,512]{2,1,0:T(4,128)(2,1)} copy(bf16[16,4,512]{2,1,0:T(4,128)(2,1)} %get-tuple-element.4) | data formatting | bytes 131072
  81.8 1.6 %copy.15 = bf16[8,64,128]{2,1,0:T(8,128)(2,1)} copy(bf16[8,64,128]{2,1,0:T(8,128)(2,1)} %get-tuple-element.5) | data formatting | bytes 262144

commit v3 on v2

--- a/solution.py
+++ b/solution.py
@@ -173,12 +173,13 @@
     shard_count, message_rows, _ = send.shape
     x_count, y_count = GRID_OF[shard_count]
     layer = y_count * CORES
-    tensor_count = gathered.shape[1]
+    tensor_count = heads.shape[0]
     request_count, step_count, _ = cross.shape
     me, mine = lax.axis_index("corpus"), lax.axis_index("tensor")
     x = me // layer
     y = (me // CORES) % y_count
     core = me % CORES
+    turn = (x + mine) % 2
 
     def device_at(dx, dy, dc):
         return (((x + dx) % x_count) * y_count + (y + dy) % y_count) * CORES + (core + dc) % CORES
@@ -224,51 +225,72 @@
 
     lax.fori_loop(1, layer, greet_layer, 0)
     lax.fori_loop(1, tensor_count, greet_tensor, 0)
-    own_weight = pltpu.make_async_copy(weight_ref, weights.at[mine, x], local_sem.at[5])
-    own_weight.start()
+    own_place = weights.at[mine // 2, x]
+    own_weight = pltpu.make_async_copy(weight_ref, own_place, local_sem.at[5])
+    pl.when(turn == 0)(own_weight.start)
     cache_copy = pltpu.make_async_copy(cache_ref, cached, local_sem.at[6])
     corpus_copy = pltpu.make_async_copy(corpus_ref, blocks, local_sem.at[7])
     cache_copy.start()
     corpus_copy.start()
+    pl.semaphore_wait(barrier, x_count - 1 + layer - 1 + tensor_count - 1)
+    for dx in range(1, x_count):
+        greet(entered, device_at(dx, 0, 0), mine)
+
+    def send_weight(dx):
+        remote(
+            weight_ref, weights.at[mine // 2, x], x_send, x_recv.at[dx], device_at(dx, 0, 0)
+        ).start()
+
+    odd_steps, even_steps = range(1, x_count, 2), range(2, x_count, 2)
+
+    @pl.when(turn == 1)
+    def _():
+        for dx in odd_steps:
+            send_weight(dx)
+
+    @pl.when(turn == 0)
+    def _():
+        for dx in even_steps:
+            send_weight(dx)
+
+    last_step, half_count = tensor_count // 2 - 1, x_count // 2
+
+    def ring_copy(down, step, offset):
+        owner = (mine + (step if down else tensor_count - step)) % tensor_count
+        piece = weights.at[owner // 2, (x + offset) % x_count]
+        after = (mine + (tensor_count - 1 if down else 1)) % tensor_count
+        return remote(
+            piece, piece, ring_send.at[down, step, offset], ring_recv.at[down, step, offset],
+            tensor=after,
+        )
+
+    def ring_ways(step, offset):
+        if step == last_step:
+            return (0,) if offset < half_count else (1,)
+        return (0, 1) if 0 <= step < last_step else ()
+
+    def ring_wait(step, offset):
+        for down in ring_ways(step, offset):
+            ring_copy(down, step, offset).wait_recv()
+
+    def ring_step(step, offset):
+        if step > last_step:
+            return
+
+        @pl.when((turn + step) % 2 == 0)
+        def _():
+            ring_wait(step - 1, offset)
+            for down in ring_ways(step, offset):
+                ring_copy(down, step, offset).start()
+
+    pl.when(turn == 0)(own_weight.wait)
+    ring_step(0, 0)
     for copy in small:
         copy.wait()
     pack_queries(shards, slots, cross, steps, columns, ranks, packed, send)
     own_query = pltpu.make_async_copy(send.at[me], arrived.at[me], query_recv.at[0])
     own_query.start()
-    pl.semaphore_wait(barrier, x_count - 1 + layer - 1 + tensor_count - 1)
-    for dx in range(1, x_count):
-        greet(entered, device_at(dx, 0, 0), mine)
-    own_weight.wait()
-
-    for dx in range(1, x_count):
-        remote(
-            weight_ref, weights.at[mine, x], x_send, x_recv.at[dx], device_at(dx, 0, 0)
-        ).start()
-    ups, downs = tensor_count // 2, (tensor_count - 1) // 2
-
-    def ring_copy(down, step, offset):
-        owner = (mine + (step if down else tensor_count - step)) % tensor_count
-        piece = weights.at[owner, (x + offset) % x_count]
-        after = (mine + (tensor_count - 1 if down else 1)) % tensor_count
-        return remote(
-            piece, piece, ring_send.at[down, step, offset], ring_recv.at[down, step, offset],
-            tensor=after,
-        )
-
-    def ring_wait(step, offset):
-        if 0 <= step < ups:
-            ring_copy(0, step, offset).wait_recv()
-        if 0 <= step < downs:
-            ring_copy(1, step, offset).wait_recv()
-
-    def ring_step(step, offset):
-        ring_wait(step - 1, offset)
-        if step < ups:
-            ring_copy(0, step, offset).start()
-        if step < downs:
-            ring_copy(1, step, offset).start()
-
-    ring_step(0, 0)
+    ring_step(1, 0)
     pl.semaphore_wait(entered, x_count - 1)
 
     def send_queries(dx, first):
@@ -291,11 +313,18 @@
             fresh_rows[index, rows, :] = fresh[request, index].astype(F32)
     cache_copy.wait()
     all_heads = range(message_rows // 8)
+
+    for offset in range(1, x_count):
+        @pl.when(turn == 0)
+        def _():
+            source = weights.at[mine // 2, (x + offset) % x_count]
+            wait_bytes(source, x_recv.at[x_count - offset])
+
+        ring_step(0, offset)
     attend_self(query_rows, fresh_rows, cached, length_ref, self_ref, all_heads[:2])
-    for offset in range(1, x_count):
-        wait_bytes(weights.at[mine, (x + offset) % x_count], x_recv.at[x_count - offset])
-        ring_step(0, offset)
+    ring_step(2, 0)
     attend_self(query_rows, fresh_rows, cached, length_ref, self_ref, all_heads[2:])
+    ring_step(1, 1)
     corpus_copy.wait()
 
     def serve(dx, carry):
@@ -312,12 +341,15 @@
             return inner
 
         lax.fori_loop(jnp.where(dx == 0, 1, 0), layer, answer, 0)
-        ring_step(1, dx)
+        if last_step > 0:
+            for index, (step, offset) in enumerate(((1, 2), (1, 3), (2, 1), (2, 2))):
+                pl.when(dx == index)(functools.partial(ring_step, step, offset))
         return carry
 
     lax.fori_loop(0, x_count, serve, 0)
     own_reply = pltpu.make_async_copy(reply.at[me], returned.at[me], reply_recv.at[0])
     own_reply.start()
+    ring_step(3, 0)
 
     def decode(dx, carry):
         first = pl.multiple_of(((x + dx) % x_count) * layer, layer)
@@ -326,7 +358,9 @@
         values = returned[chunk].astype(F32)
         sums[chunk] = values
         levels[chunk] = row_levels(values)
-        ring_step(2, dx)
+        if last_step > 1:
+            for index, (step, offset) in ((0, (2, 3)), (1, (3, 1)), (2, (3, 2)), (3, (3, 3))):
+                pl.when(dx == index)(functools.partial(ring_step, step, offset))
         return carry
 
     lax.fori_loop(0, x_count, decode, 0)
@@ -368,18 +402,28 @@
     lax.fori_loop(0, tensor_count, combine, 0)
 
     place = y * CORES + core
-    own_heads = pltpu.make_async_copy(heads.at[mine], gathered.at[place, mine], head_recv)
-    own_heads.start()
+    taker = device_at(jnp.where(x % 2 == 0, turn, x_count - turn), 0, 0)
+
+    def head_copy(owner):
+        return remote(
+            heads.at[owner], gathered.at[place, x % 2, mine // 2], head_send, head_recv,
+            taker, owner,
+        )
+
+    own_heads = pltpu.make_async_copy(
+        heads.at[mine], gathered.at[place, x % 2, mine // 2], head_recv
+    )
+    pl.when(turn == 0)(own_heads.start)
+
+    @pl.when(turn == 1)
+    def _():
+        head_copy(mine).start()
 
     def send_heads(step, carry):
-        owner = (mine + step) % tensor_count
-        remote(
-            heads.at[owner], gathered.at[place, mine], head_send, head_recv, tensor=owner
-        ).start()
+        head_copy((mine + step) % tensor_count).start()
         return carry
 
     lax.fori_loop(1, tensor_count, send_heads, 0)
-    ring_step(3, 0)
     wait_bytes(gathered.at[place], head_recv)
 
     def slot_at(dy):
@@ -395,14 +439,13 @@
 
     own = gathered.at[place]
     if y_count == 8:
-        halves = (pl.ds(0, tensor_count // 2), pl.ds(tensor_count // 2, tensor_count // 2))
+        halves = (pl.ds(0, 1), pl.ds(1, 1))
         far_low, far_high = (gathered.at[slot_at(4), half] for half in halves)
         first = [send_y(own, 2, 1), send_y(own, -2 + y_count, 3), send_y(own, 1, 0),
                  send_y(own, y_count - 1, 2)]
         for copy in first:
             copy.start()
         pass_core(place)
-        ring_step(3, 1)
         below, above = gathered.at[slot_at(y_count - 2)], gathered.at[slot_at(2)]
         wait_bytes(below, y_recv.at[1])
         second = [send_y(gathered.at[slot_at(y_count - 2), halves[0]], 2, 6), send_y(below, 1, 4)]
@@ -418,8 +461,6 @@
         for dy, number in ((y_count - 1, 0), (1, 2)):
             wait_bytes(gathered.at[slot_at(dy)], y_recv.at[number])
             pass_core(slot_at(dy))
-        ring_step(3, 2)
-        ring_step(3, 3)
         for dy, number in ((y_count - 3, 4), (3, 5)):
             wait_bytes(gathered.at[slot_at(dy)], y_recv.at[number])
             pass_core(slot_at(dy))
@@ -435,19 +476,21 @@
         for dy in range(1, y_count):
             wait_bytes(gathered.at[slot_at(y_count - dy)], y_recv.at[dy])
             pass_core(slot_at(y_count - dy))
-        for offset in range(1, x_count):
-            ring_step(3, offset)
-    for offset in range(x_count):
-        ring_wait(3, offset)
+
+    @pl.when((turn + last_step + 1) % 2 == 0)
+    def _():
+        for offset in range(x_count):
+            ring_wait(last_step, offset)
+
     wait_bytes(gathered.at[pl.ds(0, y_count)], core_recv)
 
-    half = gathered.shape[2] // 2
-    rows = layer * half
+    half = gathered.shape[3] // 2
+    rows = layer * 2 * half
 
     def project(owner):
-        block = gathered[:, owner].astype(F32)
+        block = gathered[:, :, owner].astype(F32)
         left = jnp.concatenate(
-            [block[:, :half].reshape(rows, -1), block[:, half:].reshape(rows, -1)], axis=1
+            [block[:, :, :half].reshape(rows, -1), block[:, :, half:].reshape(rows, -1)], axis=1
         ).astype(BF16)
         right = jnp.concatenate([weights[owner, index] for index in range(x_count)], axis=1)
         return jnp.dot(left, right, preferred_element_type=F32)
@@ -460,11 +503,13 @@
             totals[dx * rows : (dx + 1) * rows, :] += product[:, dx * HDIM : (dx + 1) * HDIM]
         return carry
 
-    lax.fori_loop(0, tensor_count, accumulate, 0)
-    for row in range(half):
-        for index in range(x_count):
-            picked = totals[pl.ds(index * rows + row, layer, stride=half), :]
-            out_send[index, row] = picked.astype(BF16)
+    lax.fori_loop(0, tensor_count // 2, accumulate, 0)
+    for index in range(x_count):
+        for column in range(2):
+            for row in range(half):
+                start = index * rows + column * half + row
+                picked = totals[pl.ds(start, layer, stride=2 * half), :]
+                out_send[index, column, row] = picked.astype(BF16)
     own_out = pltpu.make_async_copy(out_send.at[x], out_recv.at[x], out_recv_sem)
     own_out.start()
     for dx in range(1, x_count):
@@ -474,20 +519,39 @@
         ).start()
     wait_bytes(out_recv, out_recv_sem)
     for index in range(x_count):
-        out_ref[:, index * layer : (index + 1) * layer, :] = out_recv[index]
+        pair, column = index // 2 * 2, index % 2
+        both = out_recv[pair, column].astype(F32) + out_recv[pair + 1, column].astype(F32)
+        out_ref[:, index * layer : (index + 1) * layer, :] = both.astype(BF16)
 
     wait_bytes(send.at[pl.ds(0, shard_count - 1)], query_send)
     wait_bytes(reply.at[pl.ds(0, shard_count - 1)], reply_send)
-    wait_bytes(weights.at[mine, pl.ds(0, x_count - 1)], x_send)
-    for down, length in ((0, ups), (1, downs)):
-        for step in range(length):
+    for way, steps_sent in ((1, odd_steps), (0, even_steps)):
+        if len(steps_sent):
+            sent = weights.at[0, pl.ds(0, len(steps_sent))]
+            pl.when(turn == way)(functools.partial(wait_bytes, sent, x_send))
+    for step in range(last_step + 1):
+        @pl.when((turn + step) % 2 == 0)
+        def _():
             for offset in range(x_count):
-                ring_copy(down, step, offset).wait_send()
+                for down in ring_ways(step, offset):
+                    ring_copy(down, step, offset).wait_send()
     wait_bytes(heads.at[pl.ds(0, tensor_count - 1)], head_send)
+    pl.when(turn == 1)(functools.partial(wait_bytes, heads.at[0], head_send))
     for copy in y_copies:
         copy.wait_send()
     wait_bytes(gathered.at[pl.ds(0, y_count)], core_send)
     wait_bytes(out_send.at[pl.ds(0, x_count - 1)], out_send_sem)
+
+
+def hand_on_kernel(self_in, out_in, self_out, out_out, sems):
+    copies = [
+        pltpu.make_async_copy(self_in, self_out, sems.at[0]),
+        pltpu.make_async_copy(out_in, out_out, sems.at[1]),
+    ]
+    for copy in copies:
+        copy.start()
+    for copy in copies:
+        copy.wait()
 
 
 def on_device(
@@ -515,9 +579,9 @@
     vmem = pl.BlockSpec(memory_space=pltpu.VMEM)
     hbm = pl.BlockSpec(memory_space=pl.ANY)
     message = (shard_count, message_rows, HDIM)
-    gather_shape = (layer, tensor_count, 2 * share, width // 2)
+    gather_shape = (layer, 2, tensor_count // 2, 2 * share, width // 2)
     out_shape = (share, shard_count, out_weight.shape[1])
-    exchange = (x_count, share, layer, out_weight.shape[1])
+    exchange = (x_count, 2, share, layer, out_weight.shape[1])
     dma = pltpu.SemaphoreType.DMA
     ring_shape = (2, max(1, tensor_count // 2), x_count)
     self_heads, cross_out = pl.pallas_call(
@@ -548,10 +612,10 @@
             pltpu.VMEM(message, BF16),
             pltpu.VMEM(message, F32),
             pltpu.VMEM(message, F32),
-            pltpu.VMEM(gather_shape[1:], BF16),
+            pltpu.VMEM((tensor_count, 2 * share, width // 2), BF16),
             pltpu.VMEM(gather_shape, BF16),
-            pltpu.VMEM((tensor_count, x_count, width, HDIM), BF16),
-            pltpu.VMEM((x_count * layer * share, HDIM), F32),
+            pltpu.VMEM((tensor_count // 2, x_count, width, HDIM), BF16),
+            pltpu.VMEM((x_count * layer * 2 * share, HDIM), F32),
             pltpu.VMEM(exchange, BF16),
             pltpu.VMEM(exchange, BF16),
             pltpu.SemaphoreType.REGULAR,
@@ -573,7 +637,17 @@
         neighbour_shard.T, neighbour_slot.T, positions, kv_length,
         cross_query, self_query, step_kv, cache, corpus_kv, out_weight,
     )
-    return self_heads, cross_out
+    return pl.pallas_call(
+        hand_on_kernel,
+        out_shape=(
+            jax.ShapeDtypeStruct(self_query.shape, BF16),
+            jax.ShapeDtypeStruct(out_shape, BF16),
+        ),
+        in_specs=[vmem] * 2,
+        out_specs=(hbm, hbm),
+        scratch_shapes=[dma((2,))],
+        name="hand_on",
+    )(self_heads, cross_out)
 
 
 def solution(mesh):

time: 83.6 us -> 76.5 us (0.915)
  Pallas kernels: 79.7 us -> 75.5 us
  local copies, waits for them, and re-layouts: 3.06 us -> 0 us
    pallas_call x1, Pallas kernels: 79.7 us -> 73.9 us  [on_device(): pl.pallas_call(main_kernel, out_shape=(jax.ShapeDtypeStruct(self_query.sh...]
    unnamed x2 -> x0, local copies, waits for them, and re-layouts: 3.06 us -> none
    pallas_call x0 -> x1, Pallas kernels: none -> 1.64 us  [on_device(): pl.pallas_call(hand_on_kernel, out_shape=(jax.ShapeDtypeStruct(self_query...]
where the time goes in v3:
time: 76.5 us; the launch traced here: 76.1 us
  Pallas kernels  75.5 us (99%)
    pallas_call x1, Pallas kernels, on_device(): pl.pallas_call(main_kernel, out_shape=(jax.ShapeDtypeStruct(self_query.sh...  73.9 us
    pallas_call x1, Pallas kernels, on_device(): pl.pallas_call(hand_on_kernel, out_shape=(jax.ShapeDtypeStruct(self_query...  1.64 us

profile of v3, /device:TPU:1, one launch (start us, length us, event | category | flops | bytes accessed | tf_op | source)
XLA Modules:
  0.0 76.1 jit_solution(15141070746194733172)
XLA Ops:
  0.6 73.9 %retrieve_and_project.1 = (bf16[16,4,512]{2,1,0:T(4,128)(2,1)}, bf16[8,64,128]{2,1,0:T(8,128)(2,1)}) custom-call(s32[4,16]{1,0:T(4,128)} %bitcast.2, s32[4,16]{1,0:T(4,128)} %bitcast.3, s32[16]{0:T(128)} %position_ref.1, s32[16]{0:T(128)} %length_ref.1, bf16[16,4,512]{2,1,0:T(4,128)(2,1)} %cross_ref.1, bf16[16,4,512]{2,1,0:T(4,128)(2,1)} %query_ref.1, ...), custom_call_target="tpu_custom_call" | custom-call | tf_op jit(solution)/shard_map/retrieve_and_project/pallas_call | solution.py:587
  74.5 1.6 %hand_on.1 = (bf16[16,4,512]{2,1,0:T(4,128)(2,1)}, bf16[8,64,128]{2,1,0:T(8,128)(2,1)}) custom-call(bf16[16,4,512]{2,1,0:T(4,128)(2,1)} %get-tuple-element.4.self_in, bf16[8,64,128]{2,1,0:T(8,128)(2,1)} %get-tuple-element.5.out_in), custom_call_target="tpu_custom_call" | custom-call | tf_op jit(solution)/shard_map/hand_on/pallas_call | solution.py:640

commit v4 on v3

--- a/solution.py
+++ b/solution.py
@@ -115,36 +115,51 @@
     in_tile = lax.broadcasted_iota(jnp.int32, (source_count, 8, HDIM), 1)
     lane = lax.broadcasted_iota(jnp.int32, (source_count, 8, HDIM), 2)
     tags = jnp.where(in_tile < 3, values[:, 6:7, :], values[:, 7:8, :]).reshape(rows, HDIM)
+    tags = jnp.concatenate([tags, tags], axis=0)
     mine = [tags == F32(index + 1) for index in range(block_count)]
+    kept = [jnp.where(entry, 1.0, 0.0).astype(BF16) for entry in mine]
+    empty = jnp.zeros((rows, HDIM), F32)
     parts = []
-    for head in range(head_count):
-        lanes = slice(head * HDIM, (head + 1) * HDIM)
-        query = values[:, head * 8 : head * 8 + 8, :].reshape(rows, HDIM).astype(BF16)
-        keys = blocks[:, 0, :, lanes].reshape(block_count * token_count, HDIM)
-        scores = lax.dot_general(
-            query, keys, (((1,), (1,)), ((), ())), preferred_element_type=F32
+    for head in range(0, head_count, 2):
+        lanes = slice(head * HDIM, (head + 2) * HDIM)
+        first, second = (
+            values[:, entry * 8 : entry * 8 + 8, :].reshape(rows, HDIM) for entry in (head, head + 1)
         )
-        chosen = jnp.zeros((rows, token_count), F32)
-        for index in range(block_count):
-            chosen = jnp.where(
-                mine[index], scores[:, index * token_count : (index + 1) * token_count], chosen
+        query = jnp.concatenate(
+            [
+                jnp.concatenate([first, empty], axis=1),
+                jnp.concatenate([empty, second], axis=1),
+            ],
+            axis=0,
+        ).astype(BF16)
+        chosen = jnp.zeros((2 * rows, token_count), F32)
+        for index in range(0, block_count, 2):
+            keys = blocks[index : index + 2, 0, :, lanes].reshape(2 * token_count, 2 * HDIM)
+            scores = lax.dot_general(
+                query, keys, (((1,), (1,)), ((), ())), preferred_element_type=F32
             )
+            chosen = jnp.where(mine[index], scores[:, :token_count], chosen)
+            chosen = jnp.where(mine[index + 1], scores[:, token_count:], chosen)
         chosen = chosen * scale
         top = jnp.max(chosen, axis=1, keepdims=True)
         weights = jnp.exp(chosen - top)
         denom = jnp.sum(weights, axis=1, keepdims=True)
-        spread = jnp.concatenate(
-            [jnp.where(mine[index], weights, 0.0).astype(BF16) for index in range(block_count)], axis=1
-        )
-        held = blocks[:, 1, :, lanes].reshape(block_count * token_count, HDIM)
-        summed = jnp.dot(spread, held, preferred_element_type=F32) / denom
-        level = jnp.broadcast_to(top + jnp.log(denom), (rows, HDIM)).reshape(source_count, 8, HDIM)
-        level = jnp.sum(jnp.where(lane % 8 == in_tile, level, 0.0), axis=1, keepdims=True)
-        high = level.astype(BF16).astype(F32)
-        middle = (level - high).astype(BF16).astype(F32)
-        low = level - high - middle
-        terms = jnp.where(lane < 8, high, jnp.where(lane < 16, middle, low))
-        parts.append(jnp.where(in_tile == 6, terms, summed.reshape(source_count, 8, HDIM)))
+        low_weights = weights.astype(BF16)
+        spread = jnp.concatenate([low_weights * entry for entry in kept], axis=1)
+        held = blocks[:, 1, :, lanes].reshape(block_count * token_count, 2 * HDIM)
+        both = jnp.dot(spread, held, preferred_element_type=F32)
+        summed = jnp.concatenate([both[:rows, :HDIM], both[rows:, HDIM:]], axis=0) / denom
+        level = jnp.broadcast_to(top + jnp.log(denom), (2 * rows, HDIM))
+        for entry in range(2):
+            part = slice(entry * rows, (entry + 1) * rows)
+            mean = summed[part].reshape(source_count, 8, HDIM)
+            own = level[part].reshape(source_count, 8, HDIM)
+            own = jnp.sum(jnp.where(lane % 8 == in_tile, own, 0.0), axis=1, keepdims=True)
+            high = own.astype(BF16).astype(F32)
+            middle = (own - high).astype(BF16).astype(F32)
+            low = own - high - middle
+            terms = jnp.where(lane < 8, high, jnp.where(lane < 16, middle, low))
+            parts.append(jnp.where(in_tile == 6, terms, mean))
     return jnp.concatenate(parts, axis=1).astype(BF16)
 
 
@@ -165,7 +180,7 @@
     self_ref, out_ref,
     shards, slots, cross, query, fresh, query_rows, fresh_rows, steps, columns, ranks, packed,
     cached, blocks, send, arrived, reply, returned, sums, levels,
-    heads, gathered, weights, totals, out_send, out_recv,
+    heads, gathered, weights, left, totals, out_send, out_recv,
     entered, local_sem, query_send, query_recv, reply_send, reply_recv,
     x_send, x_recv, ring_send, ring_recv, head_send, head_recv,
     y_send, y_recv, core_send, core_recv, out_send_sem, out_recv_sem,
@@ -293,15 +308,22 @@
     ring_step(1, 0)
     pl.semaphore_wait(entered, x_count - 1)
 
+    def both_cores(dx, dy):
+        row = (((x + dx) % x_count) * y_count + (y + dy) % y_count) * CORES
+        return row + core, row + 1 - core
+
+    def send_query(target, dx):
+        remote(send.at[target], arrived.at[me], query_send, query_recv.at[dx], target).start()
+
     def send_queries(dx, first):
-        def body(step, carry):
-            target = device_at(dx, step // CORES, step % CORES)
-            remote(
-                send.at[target], arrived.at[me], query_send, query_recv.at[dx], target
-            ).start()
+        def body(dy, carry):
+            for target in both_cores(dx, dy):
+                send_query(target, dx)
             return carry
 
-        lax.fori_loop(first, layer, body, 0)
+        if first:
+            send_query(both_cores(0, 0)[1], 0)
+        lax.fori_loop(first, y_count, body, 0)
 
     for dx in range(x_count):
         send_queries(dx, 1 if dx == 0 else 0)
@@ -324,7 +346,6 @@
     attend_self(query_rows, fresh_rows, cached, length_ref, self_ref, all_heads[:2])
     ring_step(2, 0)
     attend_self(query_rows, fresh_rows, cached, length_ref, self_ref, all_heads[2:])
-    ring_step(1, 1)
     corpus_copy.wait()
 
     def serve(dx, carry):
@@ -333,23 +354,27 @@
         wait_bytes(arrived.at[chunk], query_recv.at[dx])
         reply[chunk] = attend_blocks(arrived[chunk], blocks)
 
-        def answer(step, inner):
-            target = device_at(x_count - dx, step // CORES, step % CORES)
+        def send_reply(target):
             remote(
                 reply.at[target], returned.at[me], reply_send, reply_recv.at[dx], target
             ).start()
+
+        def answer(dy, inner):
+            for target in both_cores(x_count - dx, dy):
+                send_reply(target)
             return inner
 
-        lax.fori_loop(jnp.where(dx == 0, 1, 0), layer, answer, 0)
+        pl.when(dx == 0)(lambda: send_reply(both_cores(0, 0)[1]))
+        lax.fori_loop(jnp.where(dx == 0, 1, 0), y_count, answer, 0)
         if last_step > 0:
-            for index, (step, offset) in enumerate(((1, 2), (1, 3), (2, 1), (2, 2))):
+            for index, (step, offset) in enumerate(((1, 1), (1, 2), (1, 3), (2, 1))):
                 pl.when(dx == index)(functools.partial(ring_step, step, offset))
         return carry
 
     lax.fori_loop(0, x_count, serve, 0)
     own_reply = pltpu.make_async_copy(reply.at[me], returned.at[me], reply_recv.at[0])
     own_reply.start()
-    ring_step(3, 0)
+    ring_step(2, 2)
 
     def decode(dx, carry):
         first = pl.multiple_of(((x + dx) % x_count) * layer, layer)
@@ -359,7 +384,7 @@
         sums[chunk] = values
         levels[chunk] = row_levels(values)
         if last_step > 1:
-            for index, (step, offset) in ((0, (2, 3)), (1, (3, 1)), (2, (3, 2)), (3, (3, 3))):
+            for index, (step, offset) in ((0, (2, 3)), (1, (3, 0)), (2, (3, 1))):
                 pl.when(dx == index)(functools.partial(ring_step, step, offset))
         return carry
 
@@ -390,16 +415,14 @@
         factors = [jnp.exp(entry - joint) for entry in level]
         return (factors[0] * held[0] + factors[1] * held[1]) / (factors[0] + factors[1])
 
-    def combine(owner, carry):
+    def combine(owner):
         first = combined(owner * 2)
         second = pltpu.roll(combined(owner * 2 + 1), 4, 0)
         both = jnp.where(tile_row < 4, first, second)
         upper = jnp.concatenate([both[0:8], both[8:16]], axis=1)
         lower = jnp.concatenate([both[16:24], both[24:32]], axis=1)
         heads[owner] = jnp.concatenate([upper, lower], axis=0).astype(BF16)
-        return carry
-
-    lax.fori_loop(0, tensor_count, combine, 0)
+
 
     place = y * CORES + core
     taker = device_at(jnp.where(x % 2 == 0, turn, x_count - turn), 0, 0)
@@ -413,17 +436,22 @@
     own_heads = pltpu.make_async_copy(
         heads.at[mine], gathered.at[place, x % 2, mine // 2], head_recv
     )
+
+    def send_heads(step, carry):
+        owner = (mine + step) % tensor_count
+        combine(owner)
+        head_copy(owner).start()
+        return carry
+
+    lax.fori_loop(1, tensor_count, send_heads, 0)
+    combine(mine)
     pl.when(turn == 0)(own_heads.start)
 
     @pl.when(turn == 1)
     def _():
         head_copy(mine).start()
 
-    def send_heads(step, carry):
-        head_copy((mine + step) % tensor_count).start()
-        return carry
-
-    lax.fori_loop(1, tensor_count, send_heads, 0)
+    ring_step(3, 2)
     wait_bytes(gathered.at[place], head_recv)
 
     def slot_at(dy):
@@ -439,35 +467,48 @@
 
     own = gathered.at[place]
     if y_count == 8:
-        halves = (pl.ds(0, 1), pl.ds(1, 1))
-        far_low, far_high = (gathered.at[slot_at(4), half] for half in halves)
-        first = [send_y(own, 2, 1), send_y(own, -2 + y_count, 3), send_y(own, 1, 0),
-                 send_y(own, y_count - 1, 2)]
-        for copy in first:
+        up, down = 1, y_count - 1
+
+        def half_of(index, number):
+            return gathered.at[index, pl.ds(number, 1)]
+
+        y_copies = []
+
+        def start_y(ref, dy, number):
+            copy = send_y(ref, dy, number)
             copy.start()
+            y_copies.append(copy)
+
+        for number in range(2):
+            start_y(half_of(place, number), 2, 2 + number)
+            start_y(half_of(place, 1 - number), y_count - 2, 5 - number)
+        start_y(own, up, 0)
+        start_y(own, down, 1)
         pass_core(place)
-        below, above = gathered.at[slot_at(y_count - 2)], gathered.at[slot_at(2)]
-        wait_bytes(below, y_recv.at[1])
-        second = [send_y(gathered.at[slot_at(y_count - 2), halves[0]], 2, 6), send_y(below, 1, 4)]
-        for copy in second:
-            copy.start()
-        wait_bytes(above, y_recv.at[3])
-        third = [send_y(gathered.at[slot_at(2), halves[1]], y_count - 2, 7),
-                 send_y(above, y_count - 1, 5)]
-        for copy in third:
-            copy.start()
-        pass_core(slot_at(y_count - 2))
-        pass_core(slot_at(2))
-        for dy, number in ((y_count - 1, 0), (1, 2)):
+        ring_step(3, 3)
+        below, above = slot_at(y_count - 2), slot_at(2)
+        for number in range(2):
+            low_half, high_half = half_of(below, number), half_of(above, 1 - number)
+            wait_bytes(low_half, y_recv.at[2 + number])
+            if number == 0:
+                start_y(low_half, 2, 10)
+            start_y(low_half, up, 6 + number)
+            wait_bytes(high_half, y_recv.at[5 - number])
+            if number == 0:
+                start_y(high_half, y_count - 2, 11)
+            start_y(high_half, down, 9 - number)
+        pass_core(below)
+        pass_core(above)
+        for dy, number in ((down, 0), (up, 1)):
             wait_bytes(gathered.at[slot_at(dy)], y_recv.at[number])
             pass_core(slot_at(dy))
-        for dy, number in ((y_count - 3, 4), (3, 5)):
-            wait_bytes(gathered.at[slot_at(dy)], y_recv.at[number])
+        for dy, number in ((y_count - 3, 6), (3, 8)):
+            for part in range(2):
+                wait_bytes(half_of(slot_at(dy), part), y_recv.at[number + part])
             pass_core(slot_at(dy))
-        wait_bytes(far_low, y_recv.at[6])
-        wait_bytes(far_high, y_recv.at[7])
+        wait_bytes(half_of(slot_at(4), 0), y_recv.at[10])
+        wait_bytes(half_of(slot_at(4), 1), y_recv.at[11])
         pass_core(slot_at(4))
-        y_copies = first + second + third
     else:
         y_copies = [send_y(own, dy, dy) for dy in range(1, y_count)]
         for copy in y_copies:
@@ -487,36 +528,43 @@
     half = gathered.shape[3] // 2
     rows = layer * 2 * half
 
-    def project(owner):
+    features = weights.shape[2]
+    for owner in range(tensor_count // 2):
         block = gathered[:, :, owner].astype(F32)
-        left = jnp.concatenate(
+        left[:, owner * features : (owner + 1) * features] = jnp.concatenate(
             [block[:, :, :half].reshape(rows, -1), block[:, :, half:].reshape(rows, -1)], axis=1
         ).astype(BF16)
-        right = jnp.concatenate([weights[owner, index] for index in range(x_count)], axis=1)
-        return jnp.dot(left, right, preferred_element_type=F32)
-
-    totals[...] = jnp.zeros_like(totals)
-
-    def accumulate(owner, carry):
-        product = project(owner)
-        for dx in range(x_count):
-            totals[dx * rows : (dx + 1) * rows, :] += product[:, dx * HDIM : (dx + 1) * HDIM]
-        return carry
-
-    lax.fori_loop(0, tensor_count // 2, accumulate, 0)
-    for index in range(x_count):
-        for column in range(2):
-            for row in range(half):
-                start = index * rows + column * half + row
-                picked = totals[pl.ds(start, layer, stride=2 * half), :]
-                out_send[index, column, row] = picked.astype(BF16)
-    own_out = pltpu.make_async_copy(out_send.at[x], out_recv.at[x], out_recv_sem)
-    own_out.start()
-    for dx in range(1, x_count):
-        remote(
-            out_send.at[(x + dx) % x_count], out_recv.at[x], out_send_sem, out_recv_sem,
-            device_at(dx, 0, 0),
-        ).start()
+
+    def send_out(dx):
+        target = (x + dx) % x_count
+        if dx == 0:
+            pltpu.make_async_copy(out_send.at[x], out_recv.at[x], out_recv_sem).start()
+        else:
+            remote(
+                out_send.at[target], out_recv.at[x], out_send_sem, out_recv_sem,
+                device_at(dx, 0, 0),
+            ).start()
+
+    far_first = sorted(range(x_count), key=lambda dx: -min(dx, x_count - dx))
+    for first in range(0, x_count, 2):
+        group = far_first[first : first + 2]
+        product = None
+        for owner in range(tensor_count // 2):
+            right = jnp.concatenate(
+                [weights[owner, (x + dx) % x_count] for dx in group], axis=1
+            )
+            term = jnp.dot(
+                left[:, owner * features : (owner + 1) * features], right,
+                preferred_element_type=F32,
+            )
+            product = term if product is None else product + term
+        for index, dx in enumerate(group):
+            totals[...] = product[:, index * HDIM : (index + 1) * HDIM]
+            for column in range(2):
+                for row in range(half):
+                    picked = totals[pl.ds(column * half + row, layer, stride=2 * half), :]
+                    out_send[(x + dx) % x_count, column, row] = picked.astype(BF16)
+            send_out(dx)
     wait_bytes(out_recv, out_recv_sem)
     for index in range(x_count):
         pair, column = index // 2 * 2, index % 2
@@ -615,7 +663,8 @@
             pltpu.VMEM((tensor_count, 2 * share, width // 2), BF16),
             pltpu.VMEM(gather_shape, BF16),
             pltpu.VMEM((tensor_count // 2, x_count, width, HDIM), BF16),
-            pltpu.VMEM((x_count * layer * 2 * share, HDIM), F32),
+            pltpu.VMEM((layer * 2 * share, tensor_count // 2 * width), BF16),
+            pltpu.VMEM((layer * 2 * share, HDIM), F32),
             pltpu.VMEM(exchange, BF16),
             pltpu.VMEM(exchange, BF16),
             pltpu.SemaphoreType.REGULAR,
@@ -625,7 +674,7 @@
             dma, dma((x_count,)),
             dma(ring_shape), dma(ring_shape),
             dma, dma,
-            dma((8,)), dma((8,)),
+            dma((12,)), dma((12,)),
             dma, dma,
             dma, dma,
         ],

time: 76.5 us -> 73.5 us (0.961)
  Pallas kernels: 75.5 us -> 72.7 us
    pallas_call x1, Pallas kernels: 73.9 us -> 71 us  [on_device(): pl.pallas_call(main_kernel, out_shape=(jax.ShapeDtypeStruct(self_query.sh...]
where the time goes in v4:
time: 73.5 us; the launch traced here: 73.3 us
  Pallas kernels  72.7 us (99%)
    pallas_call x1, Pallas kernels, on_device(): pl.pallas_call(main_kernel, out_shape=(jax.ShapeDtypeStruct(self_query.sh...  71 us
    pallas_call x1, Pallas kernels, on_device(): pl.pallas_call(hand_on_kernel, out_shape=(jax.ShapeDtypeStruct(self_query...  1.64 us

profile of v4, /device:TPU:1, one launch (start us, length us, event | category | flops | bytes accessed | tf_op | source)
XLA Modules:
  0.0 73.3 jit_solution(14774826507974220399)
XLA Ops:
  0.6 71.0 %retrieve_and_project.1 = (bf16[16,4,512]{2,1,0:T(4,128)(2,1)}, bf16[8,64,128]{2,1,0:T(8,128)(2,1)}) custom-call(s32[4,16]{1,0:T(4,128)} %bitcast.2, s32[4,16]{1,0:T(4,128)} %bitcast.3, s32[16]{0:T(128)} %position_ref.1, s32[16]{0:T(128)} %length_ref.1, bf16[16,4,512]{2,1,0:T(4,128)(2,1)} %cross_ref.1, bf16[16,4,512]{2,1,0:T(4,128)(2,1)} %query_ref.1, ...), custom_call_target="tpu_custom_call" | custom-call | tf_op jit(solution)/shard_map/retrieve_and_project/pallas_call | solution.py:635
  71.7 1.6 %hand_on.1 = (bf16[16,4,512]{2,1,0:T(4,128)(2,1)}, bf16[8,64,128]{2,1,0:T(8,128)(2,1)}) custom-call(bf16[16,4,512]{2,1,0:T(4,128)(2,1)} %get-tuple-element.4.self_in, bf16[8,64,128]{2,1,0:T(8,128)(2,1)} %get-tuple-element.5.out_in), custom_call_target="tpu_custom_call" | custom-call | tf_op jit(solution)/shard_map/hand_on/pallas_call | solution.py:689

commit v5 on v4

--- a/solution.py
+++ b/solution.py
@@ -306,7 +306,6 @@
     own_query = pltpu.make_async_copy(send.at[me], arrived.at[me], query_recv.at[0])
     own_query.start()
     ring_step(1, 0)
-    pl.semaphore_wait(entered, x_count - 1)
 
     def both_cores(dx, dy):
         row = (((x + dx) % x_count) * y_count + (y + dy) % y_count) * CORES
@@ -325,8 +324,10 @@
             send_query(both_cores(0, 0)[1], 0)
         lax.fori_loop(first, y_count, body, 0)
 
-    for dx in range(x_count):
-        send_queries(dx, 1 if dx == 0 else 0)
+    send_queries(0, 1)
+    pl.semaphore_wait(entered, x_count - 1)
+    for dx in range(1, x_count):
+        send_queries(dx, 0)
 
     for request in range(request_count):
         rows = slice(request * step_count, (request + 1) * step_count)
@@ -384,7 +385,7 @@
         sums[chunk] = values
         levels[chunk] = row_levels(values)
         if last_step > 1:
-            for index, (step, offset) in ((0, (2, 3)), (1, (3, 0)), (2, (3, 1))):
+            for index, (step, offset) in ((0, (2, 3)),):
                 pl.when(dx == index)(functools.partial(ring_step, step, offset))
         return carry
 
@@ -451,7 +452,6 @@
     def _():
         head_copy(mine).start()
 
-    ring_step(3, 2)
     wait_bytes(gathered.at[place], head_recv)
 
     def slot_at(dy):
@@ -485,7 +485,8 @@
         start_y(own, up, 0)
         start_y(own, down, 1)
         pass_core(place)
-        ring_step(3, 3)
+        for offset in range(x_count):
+            ring_step(3, offset)
         below, above = slot_at(y_count - 2), slot_at(2)
         for number in range(2):
             low_half, high_half = half_of(below, number), half_of(above, 1 - number)

time: 73.5 us -> 71.5 us (0.973)
  Pallas kernels: 72.7 us -> 70.7 us
    pallas_call x1, Pallas kernels: 71 us -> 69.1 us  [on_device(): pl.pallas_call(main_kernel, out_shape=(jax.ShapeDtypeStruct(self_query.sh...]
where the time goes in v5:
time: 71.5 us; the launch traced here: 71.3 us
  Pallas kernels  70.7 us (99%)
    pallas_call x1, Pallas kernels, on_device(): pl.pallas_call(main_kernel, out_shape=(jax.ShapeDtypeStruct(self_query.sh...  69.1 us
    pallas_call x1, Pallas kernels, on_device(): pl.pallas_call(hand_on_kernel, out_shape=(jax.ShapeDtypeStruct(self_query...  1.64 us

profile of v5, /device:TPU:1, one launch (start us, length us, event | category | flops | bytes accessed | tf_op | source)
XLA Modules:
  0.0 71.3 jit_solution(536656913735018553)
XLA Ops:
  0.6 69.1 %retrieve_and_project.1 = (bf16[16,4,512]{2,1,0:T(4,128)(2,1)}, bf16[8,64,128]{2,1,0:T(8,128)(2,1)}) custom-call(s32[4,16]{1,0:T(4,128)} %bitcast.2, s32[4,16]{1,0:T(4,128)} %bitcast.3, s32[16]{0:T(128)} %position_ref.1, s32[16]{0:T(128)} %length_ref.1, bf16[16,4,512]{2,1,0:T(4,128)(2,1)} %cross_ref.1, bf16[16,4,512]{2,1,0:T(4,128)(2,1)} %query_ref.1, ...), custom_call_target="tpu_custom_call" | custom-call | tf_op jit(solution)/shard_map/retrieve_and_project/pallas_call | solution.py:636
  69.7 1.6 %hand_on.1 = (bf16[16,4,512]{2,1,0:T(4,128)(2,1)}, bf16[8,64,128]{2,1,0:T(8,128)(2,1)}) custom-call(bf16[16,4,512]{2,1,0:T(4,128)(2,1)} %get-tuple-element.4.self_in, bf16[8,64,128]{2,1,0:T(8,128)(2,1)} %get-tuple-element.5.out_in), custom_call_target="tpu_custom_call" | custom-call | tf_op jit(solution)/shard_map/hand_on/pallas_call | solution.py:690

commit v6 on v5

--- a/solution.py
+++ b/solution.py
@@ -209,6 +209,9 @@
             device_id_type=MESH,
         )
 
+    def far_first_of(count, step):
+        return count // 2 + (1 - 2 * (step % 2)) * ((step + 1) // 2)
+
     def wait_bytes(ref, sem):
         pltpu.make_async_copy(ref, ref, sem).wait()
 
@@ -316,13 +319,13 @@
 
     def send_queries(dx, first):
         def body(dy, carry):
-            for target in both_cores(dx, dy):
+            for target in both_cores(dx, far_first_of(y_count, dy)):
                 send_query(target, dx)
             return carry
 
         if first:
             send_query(both_cores(0, 0)[1], 0)
-        lax.fori_loop(first, y_count, body, 0)
+        lax.fori_loop(0, y_count - first, body, 0)
 
     send_queries(0, 1)
     pl.semaphore_wait(entered, x_count - 1)
@@ -361,12 +364,12 @@
             ).start()
 
         def answer(dy, inner):
-            for target in both_cores(x_count - dx, dy):
+            for target in both_cores(x_count - dx, far_first_of(y_count, dy)):
                 send_reply(target)
             return inner
 
         pl.when(dx == 0)(lambda: send_reply(both_cores(0, 0)[1]))
-        lax.fori_loop(jnp.where(dx == 0, 1, 0), y_count, answer, 0)
+        lax.fori_loop(0, y_count - jnp.where(dx == 0, 1, 0), answer, 0)
         if last_step > 0:
             for index, (step, offset) in enumerate(((1, 1), (1, 2), (1, 3), (2, 1))):
                 pl.when(dx == index)(functools.partial(ring_step, step, offset))
@@ -439,12 +442,12 @@
     )
 
     def send_heads(step, carry):
-        owner = (mine + step) % tensor_count
+        owner = (mine + far_first_of(tensor_count, step)) % tensor_count
         combine(owner)
         head_copy(owner).start()
         return carry
 
-    lax.fori_loop(1, tensor_count, send_heads, 0)
+    lax.fori_loop(0, tensor_count - 1, send_heads, 0)
     combine(mine)
     pl.when(turn == 0)(own_heads.start)
 

time: 71.5 us -> 70.7 us (0.989)
  Pallas kernels: 70.7 us -> 69.9 us
    pallas_call x1, Pallas kernels: 69.1 us -> 68.3 us  [on_device(): pl.pallas_call(main_kernel, out_shape=(jax.ShapeDtypeStruct(self_query.sh...]
where the time goes in v6:
time: 70.7 us; the launch traced here: 70.6 us
  Pallas kernels  69.9 us (99%)
    pallas_call x1, Pallas kernels, on_device(): pl.pallas_call(main_kernel, out_shape=(jax.ShapeDtypeStruct(self_query.sh...  68.3 us
    pallas_call x1, Pallas kernels, on_device(): pl.pallas_call(hand_on_kernel, out_shape=(jax.ShapeDtypeStruct(self_query...  1.64 us

profile of v6, /device:TPU:1, one launch (start us, length us, event | category | flops | bytes accessed | tf_op | source)
XLA Modules:
  0.0 70.6 jit_solution(11365232090499983657)
XLA Ops:
  0.6 68.3 %retrieve_and_project.1 = (bf16[16,4,512]{2,1,0:T(4,128)(2,1)}, bf16[8,64,128]{2,1,0:T(8,128)(2,1)}) custom-call(s32[4,16]{1,0:T(4,128)} %bitcast.2, s32[4,16]{1,0:T(4,128)} %bitcast.3, s32[16]{0:T(128)} %position_ref.1, s32[16]{0:T(128)} %length_ref.1, bf16[16,4,512]{2,1,0:T(4,128)(2,1)} %cross_ref.1, bf16[16,4,512]{2,1,0:T(4,128)(2,1)} %query_ref.1, ...), custom_call_target="tpu_custom_call" | custom-call | tf_op jit(solution)/shard_map/retrieve_and_project/pallas_call | solution.py:639
  68.9 1.6 %hand_on.1 = (bf16[16,4,512]{2,1,0:T(4,128)(2,1)}, bf16[8,64,128]{2,1,0:T(8,128)(2,1)}) custom-call(bf16[16,4,512]{2,1,0:T(4,128)(2,1)} %get-tuple-element.4.self_in, bf16[8,64,128]{2,1,0:T(8,128)(2,1)} %get-tuple-element.5.out_in), custom_call_target="tpu_custom_call" | custom-call | tf_op jit(solution)/shard_map/hand_on/pallas_call | solution.py:693
